TPU v7x, 512 devices: a whole 4x4x16 slice. The times are simulated.
512 devices in a mesh: tok: 64 (over y, z), feat: 8 (over x, core).
Axes of the slice: x: 4, y: 4, z: 16, core: 2. Of those that a mesh axis runs over, the one named last changes fastest.
Arguments:
- activations: bfloat16 [131072, 8192], P('tok', 'feat'), may hold values from -16 to 16
- targets: bfloat16 [131072, 512], P('tok', 'feat'), may hold values from -6 to 6
Outputs:
- gram_block: float32 [8192, 512], P(('feat', 'tok'))
- cross_block: float32 [8192, 512], P(('feat', 'tok'))
All inputs are finite; a program needn't handle non-finite values.
Results may differ from a plain program's by a relative error of at most 0.0003.
Values may be sent and summed in bfloat16 or wider, within the bound.
A program may use at most 64 MiB of HBM per device.

v0:
```python
import jax
import jax.numpy as jnp
from jax import lax
from jax.sharding import PartitionSpec as P


def shifted(block, axis, distance):
    devices = range(lax.axis_size(axis))
    route = [((i - distance) % len(devices), i) for i in devices]
    return lax.ppermute(block, axis, route)


def shards(activations, targets):
    tok_rows = activations.shape[0]
    width = targets.shape[1]
    nfeat = lax.axis_size("feat")
    packed = jnp.concatenate([activations[:, :width], targets], axis=1)
    mine = lax.axis_index("feat")
    collected = jnp.zeros((tok_rows, nfeat, 2 * width), jnp.bfloat16)
    current = packed
    for step in range(nfeat):
        owner = (mine - step) % nfeat
        collected = lax.dynamic_update_slice(
            collected, current[:, None, :], (jnp.int32(0), owner, jnp.int32(0))
        )
        if step + 1 < nfeat:
            current = shifted(current, "feat", 1)
    ordered = (
        collected.reshape(tok_rows, nfeat, 2, width)
        .transpose(0, 2, 1, 3)
        .reshape(tok_rows, 2 * nfeat * width)
    )
    dims = (((0,), (0,)), ((), ()))
    term = lax.dot_general(activations, ordered, dims, preferred_element_type=jnp.float32)
    owned = lax.psum_scatter(term, "tok", scatter_dimension=0, tiled=True)
    half = nfeat * width
    return (owned[:, :half], owned[:, half:])


def solution(mesh):
    return jax.shard_map(
        shards,
        mesh=mesh,
        in_specs=(P("tok", "feat"), P("tok", "feat")),
        out_specs=(P(("feat", "tok"), None), P(("feat", "tok"), None)),
        check_vma=False,
    )
```

profile of v0, /device:TPU:1, one launch (start us, length us, event | category | flops | bytes accessed | tf_op | source)
XLA Modules:
  0.0 792.7 jit_solution(6984378771844943208)
XLA Ops:
  7.2 0.0 reduce-scatter.4.cloned.1.call-start
  7.2 1.1 slice.9
  8.3 0.2 copy.20
  8.5 1.0 pad_maximum_fusion
  9.5 2.6 collective-permute-start
  12.1 6.1 collective-permute-done
  18.3 2.5 collective-permute-start.1
  20.8 6.9 collective-permute-done.1
  27.6 1.7 collective-permute-start.2
  29.4 8.1 %collective-permute-done.2 = bf16[2048,128]{0,1:T(8,128)(2,1)S(1)} collective-permute-done((bf16[2048,128]{0,1:T(8,128)(2,1)S(1)}, bf16[2048,128]{0,1:T(8,128)(2,1)S(1)}, u32[]{:S(2)}, u32[]{:S(2)}) %collective-permute-start.2) | collective-permute-done | bytes 524320 | tf_op jit(solution)/shard_map/ppermute | solution.py:10
  37.5 0.5 collective-permute-start.3
  38.0 0.5 broadcast_in_dim.27
  38.6 8.7 %collective-permute-done.3 = bf16[2048,128]{0,1:T(8,128)(2,1)S(1)} collective-permute-done((bf16[2048,128]{0,1:T(8,128)(2,1)S(1)}, bf16[2048,128]{0,1:T(8,128)(2,1)S(1)}, u32[]{:S(2)}, u32[]{:S(2)}) %collective-permute-start.3) | collective-permute-done | bytes 524320 | tf_op jit(solution)/shard_map/ppermute | solution.py:10
  47.4 9.7 %collective-permute-done.4 = bf16[2048,128]{0,1:T(8,128)(2,1)S(1)} collective-permute-done((bf16[2048,128]{0,1:T(8,128)(2,1)S(1)}, bf16[2048,128]{0,1:T(8,128)(2,1)S(1)}, u32[]{:S(2)}, u32[]{:S(2)}) %collective-permute-start.4) | collective-permute-done | bytes 524320 | tf_op jit(solution)/shard_map/ppermute | solution.py:10
  57.2 9.7 %collective-permute-done.5 = bf16[2048,128]{0,1:T(8,128)(2,1)S(1)} collective-permute-done((bf16[2048,128]{0,1:T(8,128)(2,1)S(1)}, bf16[2048,128]{0,1:T(8,128)(2,1)S(1)}, u32[]{:S(2)}, u32[]{:S(2)}) %collective-permute-start.5) | collective-permute-done | bytes 524320 | tf_op jit(solution)/shard_map/ppermute | solution.py:10
  66.9 0.1 bitcast_dynamic-update-slice_fusion.2
  67.0 0.1 bitcast_dynamic-update-slice_fusion.1
  67.0 9.7 %collective-permute-done.6 = bf16[2048,128]{0,1:T(8,128)(2,1)S(1)} collective-permute-done((bf16[2048,128]{0,1:T(8,128)(2,1)S(1)}, bf16[2048,128]{0,1:T(8,128)(2,1)S(1)}, u32[]{:S(2)}, u32[]{:S(2)}) %collective-permute-start.6) | collective-permute-done | bytes 524320 | tf_op jit(solution)/shard_map/ppermute | solution.py:10
  76.8 0.6 copy.15
  77.4 1.6 copy-done.1
  79.0 6.0 convolution_bitcast_fusion
  85.0 5.4 copy.18
  90.4 694.1 %reduce-scatter.4.cloned.1.call-done = f32[16,1024]{1,0:T(8,128)} async-done(((f32[1024,1024]{1,0:T(8,128)}), f32[16,1024]{1,0:T(8,128)}) %reduce-scatter.4.cloned.1.call-update) | async-done | bytes 65552
  784.4 1.4 fusion
  (13 shorter events, 0.3 us)
Async XLA Ops:
  7.2 31.3 %copy-start = (bf16[2048,64]{0,1:T(8,128)(2,1)S(1)}, bf16[2048,64]{0,1:T(8,128)(2,1)}, u32[]{:S(2)}) copy-start(bf16[2048,64]{0,1:T(8,128)(2,1)} %param.3) | copy-start | bytes 786436
  7.2 777.3 %reduce-scatter.4.cloned.1.call-start = ((), (), s32[]{:S(2)}) async-start(), calls=%async_computation.1 | async-start | bytes 4259840
  9.5 8.7 %collective-permute-start = (bf16[2048,128]{0,1:T(8,128)(2,1)S(1)}, bf16[2048,128]{0,1:T(8,128)(2,1)S(1)}, u32[]{:S(2)}, u32[]{:S(2)}) collective-permute-start(bf16[2048,128]{0,1:T(8,128)(2,1)S(1)} %pad_maximum_fusion), channel_id=1, source_target_pairs={{7,0},{0,1},{1,2},{2,3},{3,4},{4,5},{5,6},{6,7},{15,8},{8,9},{9,10... | collective-permute-start | bytes 1572872 | tf_op jit(solution)/shard_map/ppermute | solution.py:10
  18.3 9.4 %collective-permute-start.1 = (bf16[2048,128]{0,1:T(8,128)(2,1)S(1)}, bf16[2048,128]{0,1:T(8,128)(2,1)S(1)}, u32[]{:S(2)}, u32[]{:S(2)}) collective-permute-start(bf16[2048,128]{0,1:T(8,128)(2,1)S(1)} %collective-permute-done), channel_id=1, source_target_pairs={{7,0},{0,1},{1,2},{2,3},{3,4},{4,5},{5,6},{6,7},{15,8},{8,9},{9,10... | collective-permute-start | bytes 1572872 | tf_op jit(solution)/shard_map/ppermute | solution.py:10
  27.6 9.8 %collective-permute-start.2 = (bf16[2048,128]{0,1:T(8,128)(2,1)S(1)}, bf16[2048,128]{0,1:T(8,128)(2,1)S(1)}, u32[]{:S(2)}, u32[]{:S(2)}) collective-permute-start(bf16[2048,128]{0,1:T(8,128)(2,1)S(1)} %collective-permute-done.1), channel_id=1, source_target_pairs={{7,0},{0,1},{1,2},{2,3},{3,4},{4,5},{5,6},{6,7},{15,8},{8,9},{9,10... | collective-permute-start | bytes 1572872 | tf_op jit(solution)/shard_map/ppermute | solution.py:10
  37.5 9.8 %collective-permute-start.3 = (bf16[2048,128]{0,1:T(8,128)(2,1)S(1)}, bf16[2048,128]{0,1:T(8,128)(2,1)S(1)}, u32[]{:S(2)}, u32[]{:S(2)}) collective-permute-start(bf16[2048,128]{0,1:T(8,128)(2,1)S(1)} %collective-permute-done.2), channel_id=1, source_target_pairs={{7,0},{0,1},{1,2},{2,3},{3,4},{4,5},{5,6},{6,7},{15,8},{8,9},{9,10... | collective-permute-start | bytes 1572872 | tf_op jit(solution)/shard_map/ppermute | solution.py:10
  47.3 9.8 %collective-permute-start.4 = (bf16[2048,128]{0,1:T(8,128)(2,1)S(1)}, bf16[2048,128]{0,1:T(8,128)(2,1)S(1)}, u32[]{:S(2)}, u32[]{:S(2)}) collective-permute-start(bf16[2048,128]{0,1:T(8,128)(2,1)S(1)} %collective-permute-done.3), channel_id=1, source_target_pairs={{7,0},{0,1},{1,2},{2,3},{3,4},{4,5},{5,6},{6,7},{15,8},{8,9},{9,10... | collective-permute-start | bytes 1572872 | tf_op jit(solution)/shard_map/ppermute | solution.py:10
  57.1 9.8 %collective-permute-start.5 = (bf16[2048,128]{0,1:T(8,128)(2,1)S(1)}, bf16[2048,128]{0,1:T(8,128)(2,1)S(1)}, u32[]{:S(2)}, u32[]{:S(2)}) collective-permute-start(bf16[2048,128]{0,1:T(8,128)(2,1)S(1)} %collective-permute-done.4), channel_id=1, source_target_pairs={{7,0},{0,1},{1,2},{2,3},{3,4},{4,5},{5,6},{6,7},{15,8},{8,9},{9,10... | collective-permute-start | bytes 1572872 | tf_op jit(solution)/shard_map/ppermute | solution.py:10
  66.9 9.8 %collective-permute-start.6 = (bf16[2048,128]{0,1:T(8,128)(2,1)S(1)}, bf16[2048,128]{0,1:T(8,128)(2,1)S(1)}, u32[]{:S(2)}, u32[]{:S(2)}) collective-permute-start(bf16[2048,128]{0,1:T(8,128)(2,1)S(1)} %collective-permute-done.5), channel_id=1, source_target_pairs={{7,0},{0,1},{1,2},{2,3},{3,4},{4,5},{5,6},{6,7},{15,8},{8,9},{9,10... | collective-permute-start | bytes 1572872 | tf_op jit(solution)/shard_map/ppermute | solution.py:10
  76.8 2.2 copy-start.1
Sparse Core Ops, SparseCore 0:
  90.5 693.8 reduce-scatter.3
where the time goes:
time: 803 us; the launch traced here: 793 us
  waiting for transfers between devices  753 us (94%)
  between operations  14.2 us (2%)
  local copies, waits for them, and re-layouts  11.1 us (1%)
    unnamed x2, waiting for transfers between devices  694 us
    ppermute x7, waiting for transfers between devices, shifted(): return lax.ppermute(block, axis, route)  58.9 us
  transfers between devices with their start and end apart: 8, of which 8 were waited for; matrix products, arithmetic and copies ran while one was open for 0% of the time, Pallas kernels for 0%

commit v1 on v0

v1 whole, which is shorter than its diff:
```python
import functools

import jax
import jax.numpy as jnp
from jax import lax
from jax.experimental import pallas as pl
from jax.experimental.pallas import tpu as pltpu
from jax.sharding import PartitionSpec as P

MESH = pl.DeviceIdType.MESH
NX, NY, ZH, ZL = 4, 4, 4, 4
OWN, LEFT, RIGHT, OPP = range(4)
PAD = 16
POWER, TOP = 12, 10.5


def packed(values):
    most = jnp.max(jnp.abs(values), axis=(0, 1), keepdims=True)
    scale = jnp.floor(TOP - jnp.log2(jnp.maximum(most, 1e-30)))
    x = values * jnp.exp2(scale)
    x2 = x * x
    x4 = x2 * x2
    code = x4 * x4 * x4
    code = jnp.where(x < 0, -code, code).astype(jnp.bfloat16)
    return code, jnp.broadcast_to(scale, (PAD, values.shape[1])).astype(jnp.bfloat16)


def unpacked(ref, rows):
    scale = ref[pl.ds(rows, PAD), :].astype(jnp.float32)[0:1]
    code = ref[pl.ds(0, rows), :].astype(jnp.float32)
    size = jnp.exp2(jnp.log2(jnp.maximum(jnp.abs(code), 1e-37)) * (1.0 / POWER) - scale)
    return jnp.where(code > 0, size, jnp.where(code < 0, -size, 0.0))


def kernel(
    sizes, a_hbm, t_hbm, gram_ref, cross_ref,
    a_ref, t_ref, at_ref, g_ref, ysend, yrecv, yown, ysum, asend, arecv, asum, brecv,
    in_sem, gs_sem, gr_sem, cs_sem, cr_sem, ys_sem, yr_sem, as_sem, ar_sem, bs_sem, br_sem,
):
    nx, ny, zh, zl = sizes
    tok, feat = lax.axis_index("tok"), lax.axis_index("feat")
    x, core = feat // 2, lax.rem(feat, 2)
    y, z = tok // (zh * zl), lax.rem(tok, zh * zl)
    h, l = z // zl, lax.rem(z, zl)
    tokens, feats = a_ref.shape
    half = tokens // 2
    width = t_ref.shape[1]
    yrows, arows, brows = feats // ny, feats // (ny * zl), feats // (ny * zl * zh)

    def at(dx=0, other=False, dy=0, dl=0, dh=0):
        xx = lax.rem(x + dx + nx, nx)
        cc = 1 - core if other else core
        yy = lax.rem(y + dy, ny)
        zz = lax.rem(h + dh, zh) * zl + lax.rem(l + dl, zl)
        return {"tok": yy * (zh * zl) + zz, "feat": xx * 2 + cc}

    first = pltpu.make_async_copy(a_hbm.at[:, pl.ds(0, 2 * width)], a_ref.at[:, pl.ds(0, 2 * width)], in_sem.at[0])
    mine = pltpu.make_async_copy(t_hbm, t_ref, in_sem.at[1])
    rest = pltpu.make_async_copy(
        a_hbm.at[:, pl.ds(2 * width, feats - 2 * width)],
        a_ref.at[:, pl.ds(2 * width, feats - 2 * width)], in_sem.at[2])
    first.start()
    mine.start()
    rest.start()

    peers = [at(other=True), at(dx=1), at(dx=-1)]
    peers += [at(dy=k) for k in range(1, ny)]
    peers += [at(dl=k) for k in range(1, zl)]
    peers += [at(dh=k) for k in range(1, zh)]
    barrier = pltpu.get_barrier_semaphore()
    for peer in peers:
        pl.semaphore_signal(barrier, inc=1, device_id=peer, device_id_type=MESH)
    pl.semaphore_wait(barrier, len(peers))

    first.wait()
    mine.wait()
    own = g_ref.at[OWN, core]
    own[:, pl.ds(0, width)] = a_ref[:, pl.ds(0, width)]
    own[:, pl.ds(width, width)] = t_ref[...]

    def remote(src, dst, send, recv, peer):
        return pltpu.make_async_remote_copy(
            src_ref=src, dst_ref=dst, send_sem=send, recv_sem=recv, device_id=peer, device_id_type=MESH)

    def rows(part):
        return pl.ds(part * half, half)

    def hop(part, direction):
        slot = LEFT if direction > 0 else RIGHT
        return remote(own.at[rows(part)], g_ref.at[slot, core, rows(part)],
                      gs_sem.at[slot, part], gr_sem.at[slot, part], at(dx=direction))

    def forward(part):
        slot, direction = (LEFT, 1) if part == 0 else (RIGHT, -1)
        return remote(g_ref.at[slot, core, rows(part)], g_ref.at[OPP, core, rows(part)],
                      gs_sem.at[OPP, part], gr_sem.at[OPP, part], at(dx=direction))

    def across(slot, part):
        block = g_ref.at[slot, core, rows(part)]
        return remote(block, block, cs_sem.at[slot, part], cr_sem.at[slot, part], at(other=True))

    def crossed(slot, part):
        block = g_ref.at[slot, 1 - core, rows(part)]
        return remote(block, block, cs_sem.at[slot, part], cr_sem.at[slot, part], at(other=True))

    hops = {(0, 1): hop(0, 1), (1, -1): hop(1, -1), (1, 1): hop(1, 1), (0, -1): hop(0, -1)}
    for copy in hops.values():
        copy.start()
    sent = list(hops.values())
    for part in range(2):
        copy = across(OWN, part)
        copy.start()
        sent.append(copy)

    rest.wait()
    tile = 128

    def transpose(i, carry):
        columns = pl.ds(pl.multiple_of(i * tile, tile), tile)
        at_ref[columns, :] = a_ref[:, columns].T
        return carry

    lax.fori_loop(0, feats // tile, transpose, 0)

    def term(stage, yy):
        block = at_ref[pl.ds(pl.multiple_of(yy * yrows, yrows), yrows), :]
        both = jnp.concatenate([g_ref[stage, 0], g_ref[stage, 1]], axis=1)
        return jnp.dot(block, both, preferred_element_type=jnp.float32)

    def ycopy(stage, k):
        return remote(ysend.at[stage, k - 1], yrecv.at[stage, k - 1],
                      ys_sem.at[stage, k - 1], yr_sem.at[stage, k - 1], at(dy=k))

    def multiply(stage):
        def step(k, carry):
            scaled, exponent = packed(term(stage, lax.rem(y + k, ny)))
            ysend[stage, k - 1, pl.ds(0, yrows), :] = scaled
            ysend[stage, k - 1, pl.ds(yrows, PAD), :] = exponent
            ycopy(stage, k).start()
            return carry

        lax.fori_loop(1, ny, step, 0)
        yown[stage] = term(stage, y)

    def acopy(stage, k):
        return remote(asend.at[stage, k - 1], arecv.at[stage, k - 1],
                      as_sem.at[stage, k - 1], ar_sem.at[stage, k - 1], at(dl=k))

    def slots(ll):
        return jnp.concatenate(
            [ysum[pl.ds(pl.multiple_of((g * zl + ll) * brows, brows), brows), :] for g in range(zh)], axis=0)

    def sum_y(stage):
        total = yown[stage]
        for k in range(1, ny):
            ycopy(stage, k).wait_recv()
            total += unpacked(yrecv.at[stage, k - 1], yrows)
        ysum[...] = total
        for k in range(1, zl):
            scaled, exponent = packed(slots(lax.rem(l + k, zl)))
            asend[stage, k - 1, pl.ds(0, arows), :] = scaled
            asend[stage, k - 1, pl.ds(arows, PAD), :] = exponent
            acopy(stage, k).start()
        asum[stage] = slots(l)

    def bcopy(stage, k):
        there = pl.ds(pl.multiple_of(lax.rem(h + k, zh) * brows, brows), brows)
        return remote(asum.at[stage, there], brecv.at[stage, k - 1],
                      bs_sem.at[stage, k - 1], br_sem.at[stage, k - 1], at(dh=k))

    def sum_a(stage):
        total = asum[stage]
        for k in range(1, zl):
            acopy(stage, k).wait_recv()
            total += unpacked(arecv.at[stage, k - 1], arows)
        asum[stage] = total
        for k in range(1, zh):
            bcopy(stage, k).start()

    def sum_b(stage):
        total = asum[stage, pl.ds(pl.multiple_of(h * brows, brows), brows), :]
        for k in range(1, zh):
            bcopy(stage, k).wait_recv()
            total += brecv[stage, k - 1]
        chip = lax.rem(x + {OWN: 0, LEFT: nx - 1, RIGHT: 1, OPP: 2}[stage], nx)
        columns = pl.ds(pl.multiple_of(chip * 2 * width, 2 * width), 2 * width)
        pieces = [total[:, i * width : (i + 1) * width] for i in range(4)]
        gram_ref[:, columns] = jnp.concatenate([pieces[0], pieces[2]], axis=1)
        cross_ref[:, columns] = jnp.concatenate([pieces[1], pieces[3]], axis=1)

    def pass_on(slot, part):
        copy = across(slot, part)
        copy.start()
        sent.append(copy)

    def go_on(part):
        copy = forward(part)
        copy.start()
        sent.append(copy)

    def get(slot):
        for part in range(2):
            crossed(slot, part).wait_recv()

    get(OWN)
    multiply(OWN)
    hops[0, 1].wait_recv()
    go_on(0)
    pass_on(LEFT, 0)
    hops[1, -1].wait_recv()
    go_on(1)
    pass_on(RIGHT, 1)
    hops[1, 1].wait_recv()
    pass_on(LEFT, 1)
    hops[0, -1].wait_recv()
    pass_on(RIGHT, 0)
    sum_y(OWN)
    get(LEFT)
    multiply(LEFT)
    get(RIGHT)
    multiply(RIGHT)
    for part in range(2):
        forward(part).wait_recv()
        pass_on(OPP, part)
    sum_a(OWN)
    get(OPP)
    multiply(OPP)
    sum_y(LEFT)
    sum_b(OWN)
    sum_y(RIGHT)
    sum_a(LEFT)
    sum_y(OPP)
    sum_a(RIGHT)
    sum_b(LEFT)
    sum_a(OPP)
    sum_b(RIGHT)
    sum_b(OPP)

    for copy in sent:
        copy.wait_send()
    for stage in range(4):
        for k in range(1, ny):
            ycopy(stage, k).wait_send()
        for k in range(1, zl):
            acopy(stage, k).wait_send()
        for k in range(1, zh):
            bcopy(stage, k).wait_send()


def shards(sizes, activations, targets):
    nx, ny, zh, zl = sizes
    tokens, feats = activations.shape
    width = targets.shape[1]
    two = 4 * width
    yrows, arows, brows = feats // ny, feats // (ny * zl), feats // (ny * zl * zh)
    out = jax.ShapeDtypeStruct((brows, nx * 2 * width), jnp.float32)
    dma = pltpu.SemaphoreType.DMA
    return pl.pallas_call(
        functools.partial(kernel, sizes),
        out_shape=(out, out),
        in_specs=[pl.BlockSpec(memory_space=pl.ANY)] * 2,
        out_specs=(pl.BlockSpec(memory_space=pltpu.VMEM),) * 2,
        scratch_shapes=[
            pltpu.VMEM((tokens, feats), jnp.bfloat16),
            pltpu.VMEM((tokens, width), jnp.bfloat16),
            pltpu.VMEM((feats, tokens), jnp.bfloat16),
            pltpu.VMEM((4, 2, tokens, 2 * width), jnp.bfloat16),
            pltpu.VMEM((4, ny - 1, yrows + PAD, two), jnp.bfloat16),
            pltpu.VMEM((4, ny - 1, yrows + PAD, two), jnp.bfloat16),
            pltpu.VMEM((4, yrows, two), jnp.float32),
            pltpu.VMEM((yrows, two), jnp.float32),
            pltpu.VMEM((4, zl - 1, arows + PAD, two), jnp.bfloat16),
            pltpu.VMEM((4, zl - 1, arows + PAD, two), jnp.bfloat16),
            pltpu.VMEM((4, arows, two), jnp.float32),
            pltpu.VMEM((4, zh - 1, brows, two), jnp.float32),
            dma((3,)),
            dma((4, 2)), dma((4, 2)),
            dma((4, 2)), dma((4, 2)),
            dma((4, ny - 1)), dma((4, ny - 1)),
            dma((4, zl - 1)), dma((4, zl - 1)),
            dma((4, zh - 1)), dma((4, zh - 1)),
        ],
        compiler_params=pltpu.CompilerParams(
            collective_id=0, has_side_effects=True, vmem_limit_bytes=48 * 1024 * 1024),
        cost_estimate=pl.CostEstimate(
            flops=2 * tokens * feats * nx * 4 * width, bytes_accessed=2 * tokens * feats, transcendentals=0),
    )(activations, targets)


def solution(mesh, sizes=(NX, NY, ZH, ZL)):
    return jax.shard_map(
        functools.partial(shards, sizes),
        mesh=mesh,
        in_specs=(P("tok", "feat"), P("tok", "feat")),
        out_specs=(P(("feat", "tok"), None), P(("feat", "tok"), None)),
        check_vma=False,
    )
```

time: 803 us -> 75.3 us (0.09); the launches traced: 793 us -> 74.2 us
  waiting for transfers between devices: 753 us -> 0 us
  Pallas kernels: 0 us -> 68.9 us
  between operations: 14.2 us -> 0.65 us
    unnamed x2 -> x0, waiting for transfers between devices: 694 us -> none
    pallas_call x0 -> x1, Pallas kernels: none -> 68.9 us  [shards(): pl.pallas_call(functools.partial(kernel, sizes), out_shape=(out, out), in...]
    ppermute x7 -> x0, waiting for transfers between devices: 58.9 us -> none  [shifted(): return lax.ppermute(block, axis, route)]
  transfers between devices with their start and end apart: 8 -> 0, of which waited for: 8 -> 0; matrix products, arithmetic and copies ran while one was open for 0% -> 0% of each run, Pallas kernels for 0% -> 0%
where the time goes in v1:
time: 75.3 us; the launch traced here: 74.2 us
  Pallas kernels  68.9 us (92%)
  local copies, waits for them, and re-layouts  4.64 us (6%)
    pallas_call x1, Pallas kernels, shards(): pl.pallas_call(functools.partial(kernel, sizes), out_shape=(out, out), in...  68.9 us
    unnamed x5, local copies, waits for them, and re-layouts  4.64 us

profile of v1, /device:TPU:1, one launch (start us, length us, event | category | flops | bytes accessed | tf_op | source)
XLA Modules:
  0.0 74.2 jit_solution(18027046763159205335)
XLA Ops:
  0.6 1.2 %copy.4.t_hbm = bf16[2048,64]{1,0:T(8,128)(2,1)S(1)} copy(bf16[2048,64]{0,1:T(8,128)(2,1)} %param.3) | data formatting | bytes 524288 | tf_op args[1]
  1.9 0.0 copy-start
  1.9 2.2 %copy-done = bf16[2048,1024]{1,0:T(8,128)(2,1)S(1)} copy-done((bf16[2048,1024]{1,0:T(8,128)(2,1)S(1)}, bf16[2048,1024]{1,0:T(8,128)(2,1)}, u32[]{:S(2)}) %copy-start) | copy-done | bytes 4194328
  4.1 68.9 %shard_map.41 = (f32[16,512]{1,0:T(8,128)S(1)}, f32[16,512]{1,0:T(8,128)S(1)}) custom-call(bf16[2048,1024]{1,0:T(8,128)(2,1)S(1)} %copy-done, bf16[2048,64]{1,0:T(8,128)(2,1)S(1)} %copy.4.t_hbm), custom_call_target="tpu_custom_call" | custom-call | flops 4294967296 | bytes 4194304 | tf_op jit(solution)/shard_map/pallas_call | solution.py:258
  73.0 0.6 copy.7
  73.6 0.6 copy.8
Async XLA Ops:
  1.9 2.2 %copy-start = (bf16[2048,1024]{1,0:T(8,128)(2,1)S(1)}, bf16[2048,1024]{1,0:T(8,128)(2,1)}, u32[]{:S(2)}) copy-start(bf16[2048,1024]{1,0:T(8,128)(2,1)} %a_hbm.1) | copy-start | bytes 12582916

commit v2 on v1

--- a/solution.py
+++ b/solution.py
@@ -10,6 +10,7 @@
 MESH = pl.DeviceIdType.MESH
 NX, NY, ZH, ZL = 4, 4, 4, 4
 OWN, LEFT, RIGHT, OPP = range(4)
+STAGES = (((OWN, 0), (OWN, 1)), ((LEFT, 0), (RIGHT, 0)), ((LEFT, 1), (RIGHT, 1)), ((OPP, 0), (OPP, 1)))
 PAD = 16
 POWER, TOP = 12, 10.5
 
@@ -34,8 +35,9 @@
 
 def kernel(
     sizes, a_hbm, t_hbm, gram_ref, cross_ref,
-    a_ref, t_ref, at_ref, g_ref, ysend, yrecv, yown, ysum, asend, arecv, asum, brecv,
-    in_sem, gs_sem, gr_sem, cs_sem, cr_sem, ys_sem, yr_sem, as_sem, ar_sem, bs_sem, br_sem,
+    a_ref, t_ref, at_ref, g_ref, ysend, yrecv, yown, ysum, asend, arecv, asum, brecv, fin,
+    in_sem, gs_sem, gr_sem, fs_sem, fr_sem, cs_sem, cr_sem, ys_sem, yr_sem, as_sem, ar_sem, bs_sem, br_sem,
+    near_sem, far_sem,
 ):
     nx, ny, zh, zl = sizes
     tok, feat = lax.axis_index("tok"), lax.axis_index("feat")
@@ -43,17 +45,17 @@
     y, z = tok // (zh * zl), lax.rem(tok, zh * zl)
     h, l = z // zl, lax.rem(z, zl)
     tokens, feats = a_ref.shape
-    half = tokens // 2
-    width = t_ref.shape[1]
+    half, quarter = tokens // 2, tokens // 4
+    width = t_ref.shape[0]
     yrows, arows, brows = feats // ny, feats // (ny * zl), feats // (ny * zl * zh)
 
-    def at(dx=0, other=False, dy=0, dl=0, dh=0):
+    def at(dx=0, dy=0, dl=0, dh=0, on=core):
         xx = lax.rem(x + dx + nx, nx)
-        cc = 1 - core if other else core
         yy = lax.rem(y + dy, ny)
         zz = lax.rem(h + dh, zh) * zl + lax.rem(l + dl, zl)
-        return {"tok": yy * (zh * zl) + zz, "feat": xx * 2 + cc}
-
+        return {"tok": yy * (zh * zl) + zz, "feat": xx * 2 + on}
+
+    partner = at(on=1 - core)
     first = pltpu.make_async_copy(a_hbm.at[:, pl.ds(0, 2 * width)], a_ref.at[:, pl.ds(0, 2 * width)], in_sem.at[0])
     mine = pltpu.make_async_copy(t_hbm, t_ref, in_sem.at[1])
     rest = pltpu.make_async_copy(
@@ -63,54 +65,95 @@
     mine.start()
     rest.start()
 
-    peers = [at(other=True), at(dx=1), at(dx=-1)]
-    peers += [at(dy=k) for k in range(1, ny)]
-    peers += [at(dl=k) for k in range(1, zl)]
-    peers += [at(dh=k) for k in range(1, zh)]
     barrier = pltpu.get_barrier_semaphore()
-    for peer in peers:
-        pl.semaphore_signal(barrier, inc=1, device_id=peer, device_id_type=MESH)
-    pl.semaphore_wait(barrier, len(peers))
+    near = [dict(dx=1), dict(dx=-1)] + [dict(dy=k) for k in range(1, ny)]
+    far = [dict(dl=k) for k in range(1, zl)] + [dict(dh=k) for k in range(1, zh)]
+    for there in near:
+        pl.semaphore_signal(barrier, inc=1, device_id=at(on=1, **there), device_id_type=MESH)
+    for there in far:
+        pl.semaphore_signal(barrier, inc=1, device_id=at(on=0, **there), device_id_type=MESH)
+
+    @pl.when(core == 0)
+    def _():
+        pl.semaphore_signal(barrier, inc=1, device_id=partner, device_id_type=MESH)
+
+    @pl.when(core == 1)
+    def _():
+        pl.semaphore_wait(barrier, 2 * len(near) + 1)
+        pl.semaphore_signal(near_sem, inc=1, device_id=partner, device_id_type=MESH)
+
+    @pl.when(core == 0)
+    def _():
+        pl.semaphore_wait(near_sem, 1)
+
+    def meet_far():
+        @pl.when(core == 0)
+        def _():
+            pl.semaphore_wait(barrier, 2 * len(far))
+            pl.semaphore_signal(far_sem, inc=1, device_id=partner, device_id_type=MESH)
+
+        @pl.when(core == 1)
+        def _():
+            pl.semaphore_wait(far_sem, 1)
 
     first.wait()
     mine.wait()
     own = g_ref.at[OWN, core]
     own[:, pl.ds(0, width)] = a_ref[:, pl.ds(0, width)]
-    own[:, pl.ds(width, width)] = t_ref[...]
+    own[:, pl.ds(width, width)] = t_ref[...].T
 
     def remote(src, dst, send, recv, peer):
         return pltpu.make_async_remote_copy(
             src_ref=src, dst_ref=dst, send_sem=send, recv_sem=recv, device_id=peer, device_id_type=MESH)
 
     def rows(part):
-        return pl.ds(part * half, half)
-
-    def hop(part, direction):
-        slot = LEFT if direction > 0 else RIGHT
-        return remote(own.at[rows(part)], g_ref.at[slot, core, rows(part)],
-                      gs_sem.at[slot, part], gr_sem.at[slot, part], at(dx=direction))
-
-    def forward(part):
-        slot, direction = (LEFT, 1) if part == 0 else (RIGHT, -1)
-        return remote(g_ref.at[slot, core, rows(part)], g_ref.at[OPP, core, rows(part)],
-                      gs_sem.at[OPP, part], gr_sem.at[OPP, part], at(dx=direction))
-
-    def across(slot, part):
-        block = g_ref.at[slot, core, rows(part)]
-        return remote(block, block, cs_sem.at[slot, part], cr_sem.at[slot, part], at(other=True))
-
-    def crossed(slot, part):
-        block = g_ref.at[slot, 1 - core, rows(part)]
-        return remote(block, block, cs_sem.at[slot, part], cr_sem.at[slot, part], at(other=True))
-
-    hops = {(0, 1): hop(0, 1), (1, -1): hop(1, -1), (1, 1): hop(1, 1), (0, -1): hop(0, -1)}
-    for copy in hops.values():
-        copy.start()
-    sent = list(hops.values())
-    for part in range(2):
-        copy = across(OWN, part)
-        copy.start()
-        sent.append(copy)
+        return pl.ds(pl.multiple_of(part * half, half), half)
+
+    def rows4(part, q):
+        return pl.ds(pl.multiple_of(part * half + q * quarter, quarter), quarter)
+
+    def hop(slot, b):
+        return remote(g_ref.at[OWN, b, rows(core)], g_ref.at[slot, b, rows(core)],
+                      gs_sem.at[slot - 1, b], gr_sem.at[slot - 1, b], at(dx=1 if slot == LEFT else -1))
+
+    def forward(slot, b):
+        part = rows4(core, slot - 1)
+        return remote(g_ref.at[slot, b, part], g_ref.at[OPP, b, part],
+                      fs_sem.at[slot - 1, b], fr_sem.at[slot - 1, b], at(dx=1 if slot == LEFT else -1))
+
+    def share(part):
+        block = g_ref.at[OWN, core, rows(part)]
+        return remote(block, block, cs_sem.at[OWN, part], cr_sem.at[OWN, part], partner)
+
+    def shared(part):
+        block = g_ref.at[OWN, 1 - core, rows(part)]
+        return remote(block, block, cs_sem.at[OWN, part], cr_sem.at[OWN, part], partner)
+
+    def across(slot, b):
+        block = g_ref.at[slot, b, rows(core)]
+        return remote(block, block, cs_sem.at[slot, b], cr_sem.at[slot, b], partner)
+
+    def crossed(slot, b):
+        block = g_ref.at[slot, b, rows(1 - core)]
+        return remote(block, block, cs_sem.at[slot, b], cr_sem.at[slot, b], partner)
+
+    share(1 - core).start()
+    share(core).start()
+
+    @pl.when(core == 0)
+    def _():
+        hop(LEFT, 0).start()
+        hop(RIGHT, 0).start()
+
+    shared(core).wait_recv()
+
+    @pl.when(core == 1)
+    def _():
+        hop(LEFT, 0).start()
+        hop(RIGHT, 0).start()
+
+    hop(LEFT, 1).start()
+    hop(RIGHT, 1).start()
 
     rest.wait()
     tile = 128
@@ -124,7 +167,7 @@
 
     def term(stage, yy):
         block = at_ref[pl.ds(pl.multiple_of(yy * yrows, yrows), yrows), :]
-        both = jnp.concatenate([g_ref[stage, 0], g_ref[stage, 1]], axis=1)
+        both = jnp.concatenate([g_ref[slot, b] for slot, b in STAGES[stage]], axis=1)
         return jnp.dot(block, both, preferred_element_type=jnp.float32)
 
     def ycopy(stage, k):
@@ -156,6 +199,8 @@
             ycopy(stage, k).wait_recv()
             total += unpacked(yrecv.at[stage, k - 1], yrows)
         ysum[...] = total
+        if stage == 0:
+            meet_far()
         for k in range(1, zl):
             scaled, exponent = packed(slots(lax.rem(l + k, zl)))
             asend[stage, k - 1, pl.ds(0, arows), :] = scaled
@@ -182,62 +227,64 @@
         for k in range(1, zh):
             bcopy(stage, k).wait_recv()
             total += brecv[stage, k - 1]
-        chip = lax.rem(x + {OWN: 0, LEFT: nx - 1, RIGHT: 1, OPP: 2}[stage], nx)
+        fin[stage] = total
+
+    def finish(shift, places):
+        chip = lax.rem(x + shift, nx)
         columns = pl.ds(pl.multiple_of(chip * 2 * width, 2 * width), 2 * width)
-        pieces = [total[:, i * width : (i + 1) * width] for i in range(4)]
-        gram_ref[:, columns] = jnp.concatenate([pieces[0], pieces[2]], axis=1)
-        cross_ref[:, columns] = jnp.concatenate([pieces[1], pieces[3]], axis=1)
-
-    def pass_on(slot, part):
-        copy = across(slot, part)
-        copy.start()
-        sent.append(copy)
-
-    def go_on(part):
-        copy = forward(part)
-        copy.start()
-        sent.append(copy)
-
-    def get(slot):
-        for part in range(2):
-            crossed(slot, part).wait_recv()
-
-    get(OWN)
-    multiply(OWN)
-    hops[0, 1].wait_recv()
-    go_on(0)
-    pass_on(LEFT, 0)
-    hops[1, -1].wait_recv()
-    go_on(1)
-    pass_on(RIGHT, 1)
-    hops[1, 1].wait_recv()
-    pass_on(LEFT, 1)
-    hops[0, -1].wait_recv()
-    pass_on(RIGHT, 0)
-    sum_y(OWN)
-    get(LEFT)
-    multiply(LEFT)
-    get(RIGHT)
-    multiply(RIGHT)
+        for out, skip in ((gram_ref, 0), (cross_ref, width)):
+            out[:, columns] = jnp.concatenate(
+                [fin[stage][:, side * 2 * width + skip : side * 2 * width + skip + width] for stage, side in places],
+                axis=1)
+
+    def take(b):
+        for slot in (LEFT, RIGHT):
+            hop(slot, b).wait_recv()
+            across(slot, b).start()
+            forward(slot, b).start()
+
+    shared(1 - core).wait_recv()
+    multiply(0)
+    take(0)
+    for slot in (LEFT, RIGHT):
+        crossed(slot, 0).wait_recv()
+    multiply(1)
+    sum_y(0)
+    take(1)
+    for slot in (LEFT, RIGHT):
+        crossed(slot, 1).wait_recv()
+    multiply(2)
+    sum_a(0)
+    for b in range(2):
+        for slot in (LEFT, RIGHT):
+            forward(slot, b).wait_recv()
+        across(OPP, b).start()
+    sum_y(1)
+    for b in range(2):
+        crossed(OPP, b).wait_recv()
+    multiply(3)
+    sum_y(2)
+    sum_a(1)
+    sum_b(0)
+    finish(0, ((0, 0), (0, 1)))
+    sum_a(2)
+    sum_y(3)
+    sum_b(1)
+    sum_b(2)
+    finish(nx - 1, ((1, 0), (2, 0)))
+    finish(1, ((1, 1), (2, 1)))
+    sum_a(3)
+    sum_b(3)
+    finish(nx // 2, ((3, 0), (3, 1)))
+
     for part in range(2):
-        forward(part).wait_recv()
-        pass_on(OPP, part)
-    sum_a(OWN)
-    get(OPP)
-    multiply(OPP)
-    sum_y(LEFT)
-    sum_b(OWN)
-    sum_y(RIGHT)
-    sum_a(LEFT)
-    sum_y(OPP)
-    sum_a(RIGHT)
-    sum_b(LEFT)
-    sum_a(OPP)
-    sum_b(RIGHT)
-    sum_b(OPP)
-
-    for copy in sent:
-        copy.wait_send()
+        share(part).wait_send()
+    for b in range(2):
+        for slot in (LEFT, RIGHT):
+            hop(slot, b).wait_send()
+            forward(slot, b).wait_send()
+        for slot in (LEFT, RIGHT, OPP):
+            across(slot, b).wait_send()
     for stage in range(4):
         for k in range(1, ny):
             ycopy(stage, k).wait_send()
@@ -262,7 +309,7 @@
         out_specs=(pl.BlockSpec(memory_space=pltpu.VMEM),) * 2,
         scratch_shapes=[
             pltpu.VMEM((tokens, feats), jnp.bfloat16),
-            pltpu.VMEM((tokens, width), jnp.bfloat16),
+            pltpu.VMEM((width, tokens), jnp.bfloat16),
             pltpu.VMEM((feats, tokens), jnp.bfloat16),
             pltpu.VMEM((4, 2, tokens, 2 * width), jnp.bfloat16),
             pltpu.VMEM((4, ny - 1, yrows + PAD, two), jnp.bfloat16),
@@ -273,18 +320,21 @@
             pltpu.VMEM((4, zl - 1, arows + PAD, two), jnp.bfloat16),
             pltpu.VMEM((4, arows, two), jnp.float32),
             pltpu.VMEM((4, zh - 1, brows, two), jnp.float32),
+            pltpu.VMEM((4, brows, two), jnp.float32),
             dma((3,)),
-            dma((4, 2)), dma((4, 2)),
+            dma((2, 2)), dma((2, 2)),
+            dma((2, 2)), dma((2, 2)),
             dma((4, 2)), dma((4, 2)),
             dma((4, ny - 1)), dma((4, ny - 1)),
             dma((4, zl - 1)), dma((4, zl - 1)),
             dma((4, zh - 1)), dma((4, zh - 1)),
+            pltpu.SemaphoreType.REGULAR, pltpu.SemaphoreType.REGULAR,
         ],
         compiler_params=pltpu.CompilerParams(
-            collective_id=0, has_side_effects=True, vmem_limit_bytes=48 * 1024 * 1024),
+            collective_id=0, has_side_effects=True, vmem_limit_bytes=60 * 1024 * 1024),
         cost_estimate=pl.CostEstimate(
             flops=2 * tokens * feats * nx * 4 * width, bytes_accessed=2 * tokens * feats, transcendentals=0),
-    )(activations, targets)
+    )(activations, targets.T)
 
 
 def solution(mesh, sizes=(NX, NY, ZH, ZL)):

time: 75.3 us -> 68.1 us (0.904)
  Pallas kernels: 68.9 us -> 63.9 us
  local copies, waits for them, and re-layouts: 4.64 us -> 2.75 us
    pallas_call x1, Pallas kernels: 68.9 us -> 63.9 us  [shards(): pl.pallas_call(functools.partial(kernel, sizes), out_shape=(out, out), in...]
    unnamed x5 -> x2, local copies, waits for them, and re-layouts: 4.64 us -> 2.75 us
where the time goes in v2:
time: 68.1 us; the launch traced here: 67.3 us
  Pallas kernels  63.9 us (94%)
  local copies, waits for them, and re-layouts  2.75 us (4%)
    pallas_call x1, Pallas kernels, shards(): pl.pallas_call(functools.partial(kernel, sizes), out_shape=(out, out), in...  63.9 us
    unnamed x2, local copies, waits for them, and re-layouts  2.75 us

profile of v2, /device:TPU:1, one launch (start us, length us, event | category | flops | bytes accessed | tf_op | source)
XLA Modules:
  0.0 67.3 jit_solution(5120958879235059217)
XLA Ops:
  0.6 63.9 %shard_map.41 = (f32[16,512]{1,0:T(8,128)}, f32[16,512]{1,0:T(8,128)}) custom-call(bf16[2048,1024]{1,0:T(8,128)(2,1)} %a_hbm.1, bf16[64,2048]{1,0:T(8,128)(2,1)} %bitcast.1), custom_call_target="tpu_custom_call" | custom-call | flops 4294967296 | bytes 4194304 | tf_op jit(solution)/shard_map/pallas_call | solution.py:305
  64.6 1.4 %copy.6 = f32[16,512]{1,0:T(8,128)} copy(f32[16,512]{1,0:T(8,128)} %get-tuple-element.4) | data formatting | bytes 65536
  66.0 1.4 %copy.7 = f32[16,512]{1,0:T(8,128)} copy(f32[16,512]{1,0:T(8,128)} %get-tuple-element.5) | data formatting | bytes 65536

commit v3 on v2

--- a/solution.py
+++ b/solution.py
@@ -11,6 +11,7 @@
 NX, NY, ZH, ZL = 4, 4, 4, 4
 OWN, LEFT, RIGHT, OPP = range(4)
 STAGES = (((OWN, 0), (OWN, 1)), ((LEFT, 0), (RIGHT, 0)), ((LEFT, 1), (RIGHT, 1)), ((OPP, 0), (OPP, 1)))
+PIECES = ((0, 0, ZH), (1, 0, ZH), (2, 0, ZH // 2), (2, ZH // 2, ZH // 2), (3, 0, 1), (3, 1, 1), (3, 2, ZH - 2))
 PAD = 16
 POWER, TOP = 12, 10.5
 
@@ -165,69 +166,103 @@
 
     lax.fori_loop(0, feats // tile, transpose, 0)
 
-    def term(stage, yy):
-        block = at_ref[pl.ds(pl.multiple_of(yy * yrows, yrows), yrows), :]
+    def ycopy(p, k):
+        part = pl.ds(0, PIECES[p][2] * zl * brows + PAD)
+        return remote(ysend.at[p, k - 1, part], yrecv.at[p, k - 1, part],
+                      ys_sem.at[p, k - 1], yr_sem.at[p, k - 1], at(dy=k))
+
+    def multiply(p):
+        stage, low, count = PIECES[p]
+        size = count * zl * brows
         both = jnp.concatenate([g_ref[slot, b] for slot, b in STAGES[stage]], axis=1)
-        return jnp.dot(block, both, preferred_element_type=jnp.float32)
-
-    def ycopy(stage, k):
-        return remote(ysend.at[stage, k - 1], yrecv.at[stage, k - 1],
-                      ys_sem.at[stage, k - 1], yr_sem.at[stage, k - 1], at(dy=k))
-
-    def multiply(stage):
-        def step(k, carry):
-            scaled, exponent = packed(term(stage, lax.rem(y + k, ny)))
-            ysend[stage, k - 1, pl.ds(0, yrows), :] = scaled
-            ysend[stage, k - 1, pl.ds(yrows, PAD), :] = exponent
-            ycopy(stage, k).start()
-            return carry
-
-        lax.fori_loop(1, ny, step, 0)
-        yown[stage] = term(stage, y)
-
-    def acopy(stage, k):
-        return remote(asend.at[stage, k - 1], arecv.at[stage, k - 1],
-                      as_sem.at[stage, k - 1], ar_sem.at[stage, k - 1], at(dl=k))
-
-    def slots(ll):
+        order = [2, 1, 3, 0] if ny == 4 else [*range(1, ny), 0]
+        at_once = yrows // size
+        for first_k in range(0, ny, at_once):
+            group = order[first_k : first_k + at_once]
+            block = jnp.concatenate(
+                [at_ref[pl.ds(pl.multiple_of(lax.rem(y + k, ny) * yrows + low * zl * brows, zl * brows), size), :]
+                 for k in group], axis=0)
+            terms = jnp.dot(block, both, preferred_element_type=jnp.float32)
+            for i, k in enumerate(group):
+                term = terms[i * size : (i + 1) * size]
+                if k == 0:
+                    yown[p, pl.ds(0, size), :] = term
+                    continue
+                code, exponent = packed(term)
+                ysend[p, k - 1, pl.ds(0, size), :] = code
+                ysend[p, k - 1, pl.ds(size, PAD), :] = exponent
+                ycopy(p, k).start()
+
+    def acopy(p, k):
+        part = pl.ds(0, PIECES[p][2] * brows + PAD)
+        return remote(asend.at[p, k - 1, part], arecv.at[p, k - 1, part],
+                      as_sem.at[p, k - 1], ar_sem.at[p, k - 1], at(dl=k))
+
+    def slots(p, ll):
         return jnp.concatenate(
-            [ysum[pl.ds(pl.multiple_of((g * zl + ll) * brows, brows), brows), :] for g in range(zh)], axis=0)
-
-    def sum_y(stage):
-        total = yown[stage]
+            [ysum[pl.ds(pl.multiple_of((g * zl + ll) * brows, brows), brows), :] for g in range(PIECES[p][2])], axis=0)
+
+    def sum_y(p):
+        size, asize = PIECES[p][2] * zl * brows, PIECES[p][2] * brows
+        total = yown[p, pl.ds(0, size), :]
         for k in range(1, ny):
-            ycopy(stage, k).wait_recv()
-            total += unpacked(yrecv.at[stage, k - 1], yrows)
-        ysum[...] = total
-        if stage == 0:
+            ycopy(p, k).wait_recv()
+            total += unpacked(yrecv.at[p, k - 1], size)
+        ysum[pl.ds(0, size), :] = total
+        if p == 0:
             meet_far()
         for k in range(1, zl):
-            scaled, exponent = packed(slots(lax.rem(l + k, zl)))
-            asend[stage, k - 1, pl.ds(0, arows), :] = scaled
-            asend[stage, k - 1, pl.ds(arows, PAD), :] = exponent
-            acopy(stage, k).start()
-        asum[stage] = slots(l)
-
-    def bcopy(stage, k):
-        there = pl.ds(pl.multiple_of(lax.rem(h + k, zh) * brows, brows), brows)
-        return remote(asum.at[stage, there], brecv.at[stage, k - 1],
-                      bs_sem.at[stage, k - 1], br_sem.at[stage, k - 1], at(dh=k))
-
-    def sum_a(stage):
-        total = asum[stage]
+            code, exponent = packed(slots(p, lax.rem(l + k, zl)))
+            asend[p, k - 1, pl.ds(0, asize), :] = code
+            asend[p, k - 1, pl.ds(asize, PAD), :] = exponent
+            acopy(p, k).start()
+        asum[p, pl.ds(0, asize), :] = slots(p, l)
+
+    def inside(p, g):
+        _, low, count = PIECES[p]
+        return (g >= low) & (g < low + count)
+
+    def bcopy(p, k):
+        _, low, count = PIECES[p]
+        there = lax.rem(lax.rem(h + k, zh) - low + zh, zh)
+        if count == 1:
+            there = 0
+        part = pl.ds(pl.multiple_of(there * brows, brows), brows)
+        return remote(asum.at[p, part], brecv.at[p, k - 1], bs_sem.at[p, k - 1], br_sem.at[p, k - 1], at(dh=k))
+
+    def brecvd(p, k):
+        part = pl.ds(0, brows)
+        return remote(asum.at[p, part], brecv.at[p, k - 1], bs_sem.at[p, k - 1], br_sem.at[p, k - 1], at(dh=k))
+
+    def sum_a(p):
+        asize = PIECES[p][2] * brows
+        total = asum[p, pl.ds(0, asize), :]
         for k in range(1, zl):
-            acopy(stage, k).wait_recv()
-            total += unpacked(arecv.at[stage, k - 1], arows)
-        asum[stage] = total
+            acopy(p, k).wait_recv()
+            total += unpacked(arecv.at[p, k - 1], asize)
+        asum[p, pl.ds(0, asize), :] = total
         for k in range(1, zh):
-            bcopy(stage, k).start()
-
-    def sum_b(stage):
-        total = asum[stage, pl.ds(pl.multiple_of(h * brows, brows), brows), :]
+            @pl.when(inside(p, lax.rem(h + k, zh)))
+            def _():
+                bcopy(p, k).start()
+
+    def sum_b(p):
+        stage, low, count = PIECES[p]
+
+        @pl.when(inside(p, h))
+        def _():
+            mine = lax.rem(h - low + zh, zh) if count > 1 else 0
+            total = asum[p, pl.ds(pl.multiple_of(mine * brows, brows), brows), :]
+            for k in range(1, zh):
+                brecvd(p, k).wait_recv()
+                total += brecv[p, k - 1]
+            fin[stage] = total
+
+    def sent_b(p):
         for k in range(1, zh):
-            bcopy(stage, k).wait_recv()
-            total += brecv[stage, k - 1]
-        fin[stage] = total
+            @pl.when(inside(p, lax.rem(h + k, zh)))
+            def _():
+                brecvd(p, k).wait_send()
 
     def finish(shift, places):
         chip = lax.rem(x + shift, nx)
@@ -254,6 +289,7 @@
     for slot in (LEFT, RIGHT):
         crossed(slot, 1).wait_recv()
     multiply(2)
+    multiply(3)
     sum_a(0)
     for b in range(2):
         for slot in (LEFT, RIGHT):
@@ -262,19 +298,30 @@
     sum_y(1)
     for b in range(2):
         crossed(OPP, b).wait_recv()
-    multiply(3)
+    multiply(4)
+    multiply(5)
+    multiply(6)
     sum_y(2)
     sum_a(1)
     sum_b(0)
+    sum_y(3)
+    sum_y(4)
+    sum_a(2)
+    sum_y(5)
+    sum_a(3)
+    sum_a(4)
+    sum_y(6)
+    sum_a(5)
+    sum_b(1)
     finish(0, ((0, 0), (0, 1)))
-    sum_a(2)
-    sum_y(3)
-    sum_b(1)
+    sum_a(6)
     sum_b(2)
+    sum_b(3)
     finish(nx - 1, ((1, 0), (2, 0)))
     finish(1, ((1, 1), (2, 1)))
-    sum_a(3)
-    sum_b(3)
+    sum_b(4)
+    sum_b(5)
+    sum_b(6)
     finish(nx // 2, ((3, 0), (3, 1)))
 
     for part in range(2):
@@ -285,20 +332,19 @@
             forward(slot, b).wait_send()
         for slot in (LEFT, RIGHT, OPP):
             across(slot, b).wait_send()
-    for stage in range(4):
+    for p in range(len(PIECES)):
         for k in range(1, ny):
-            ycopy(stage, k).wait_send()
+            ycopy(p, k).wait_send()
         for k in range(1, zl):
-            acopy(stage, k).wait_send()
-        for k in range(1, zh):
-            bcopy(stage, k).wait_send()
+            acopy(p, k).wait_send()
+        sent_b(p)
 
 
 def shards(sizes, activations, targets):
     nx, ny, zh, zl = sizes
     tokens, feats = activations.shape
     width = targets.shape[1]
-    two = 4 * width
+    two, n = 4 * width, len(PIECES)
     yrows, arows, brows = feats // ny, feats // (ny * zl), feats // (ny * zl * zh)
     out = jax.ShapeDtypeStruct((brows, nx * 2 * width), jnp.float32)
     dma = pltpu.SemaphoreType.DMA
@@ -312,26 +358,26 @@
             pltpu.VMEM((width, tokens), jnp.bfloat16),
             pltpu.VMEM((feats, tokens), jnp.bfloat16),
             pltpu.VMEM((4, 2, tokens, 2 * width), jnp.bfloat16),
-            pltpu.VMEM((4, ny - 1, yrows + PAD, two), jnp.bfloat16),
-            pltpu.VMEM((4, ny - 1, yrows + PAD, two), jnp.bfloat16),
-            pltpu.VMEM((4, yrows, two), jnp.float32),
+            pltpu.VMEM((n, ny - 1, yrows + PAD, two), jnp.bfloat16),
+            pltpu.VMEM((n, ny - 1, yrows + PAD, two), jnp.bfloat16),
+            pltpu.VMEM((n, yrows, two), jnp.float32),
             pltpu.VMEM((yrows, two), jnp.float32),
-            pltpu.VMEM((4, zl - 1, arows + PAD, two), jnp.bfloat16),
-            pltpu.VMEM((4, zl - 1, arows + PAD, two), jnp.bfloat16),
-            pltpu.VMEM((4, arows, two), jnp.float32),
-            pltpu.VMEM((4, zh - 1, brows, two), jnp.float32),
+            pltpu.VMEM((n, zl - 1, arows + PAD, two), jnp.bfloat16),
+            pltpu.VMEM((n, zl - 1, arows + PAD, two), jnp.bfloat16),
+            pltpu.VMEM((n, arows, two), jnp.float32),
+            pltpu.VMEM((n, zh - 1, brows, two), jnp.float32),
             pltpu.VMEM((4, brows, two), jnp.float32),
             dma((3,)),
             dma((2, 2)), dma((2, 2)),
             dma((2, 2)), dma((2, 2)),
             dma((4, 2)), dma((4, 2)),
-            dma((4, ny - 1)), dma((4, ny - 1)),
-            dma((4, zl - 1)), dma((4, zl - 1)),
-            dma((4, zh - 1)), dma((4, zh - 1)),
+            dma((n, ny - 1)), dma((n, ny - 1)),
+            dma((n, zl - 1)), dma((n, zl - 1)),
+            dma((n, zh - 1)), dma((n, zh - 1)),
             pltpu.SemaphoreType.REGULAR, pltpu.SemaphoreType.REGULAR,
         ],
         compiler_params=pltpu.CompilerParams(
-            collective_id=0, has_side_effects=True, vmem_limit_bytes=60 * 1024 * 1024),
+            collective_id=0, has_side_effects=True, vmem_limit_bytes=53 * 1024 * 1024),
         cost_estimate=pl.CostEstimate(
             flops=2 * tokens * feats * nx * 4 * width, bytes_accessed=2 * tokens * feats, transcendentals=0),
     )(activations, targets.T)

time: 68.1 us -> 66 us (0.969)
  the two profiles are of different devices: /device:TPU:1 before, /device:TPU:224 now
where the time goes in v3:
time: 66 us; the launch traced here: 65.8 us
  Pallas kernels  63 us (95%)
  local copies, waits for them, and re-layouts  2.17 us (3%)
    pallas_call x1, Pallas kernels, shards(): pl.pallas_call(functools.partial(kernel, sizes), out_shape=(out, out), in...  63 us
    unnamed x4, local copies, waits for them, and re-layouts  2.17 us

profile of v3, /device:TPU:224, one launch (start us, length us, event | category | flops | bytes accessed | tf_op | source)
XLA Modules:
  0.0 65.8 jit_solution(2777503036339549595)
XLA Ops:
  0.6 0.0 copy-start
  0.6 0.9 %copy-done = bf16[2048,64]{0,1:T(8,128)(2,1)S(1)} copy-done((bf16[2048,64]{0,1:T(8,128)(2,1)S(1)}, bf16[2048,64]{0,1:T(8,128)(2,1)}, u32[]{:S(2)}) %copy-start) | copy-done | bytes 262168
  1.6 63.0 %shard_map.41 = (f32[16,512]{1,0:T(8,128)S(1)}, f32[16,512]{1,0:T(8,128)S(1)}) custom-call(bf16[2048,1024]{1,0:T(8,128)(2,1)} %a_hbm.1, bf16[64,2048]{1,0:T(8,128)(2,1)S(1)} %bitcast.1), custom_call_target="tpu_custom_call" | custom-call | flops 4294967296 | bytes 4194304 | tf_op jit(solution)/shard_map/pallas_call | solution.py:351
  64.6 0.6 copy.6
  65.2 0.6 copy.7
Async XLA Ops:
  0.6 1.0 %copy-start = (bf16[2048,64]{0,1:T(8,128)(2,1)S(1)}, bf16[2048,64]{0,1:T(8,128)(2,1)}, u32[]{:S(2)}) copy-start(bf16[2048,64]{0,1:T(8,128)(2,1)} %param.3) | copy-start | bytes 786436

commit v4 on v3

--- a/solution.py
+++ b/solution.py
@@ -12,7 +12,7 @@
 OWN, LEFT, RIGHT, OPP = range(4)
 STAGES = (((OWN, 0), (OWN, 1)), ((LEFT, 0), (RIGHT, 0)), ((LEFT, 1), (RIGHT, 1)), ((OPP, 0), (OPP, 1)))
 PIECES = ((0, 0, ZH), (1, 0, ZH), (2, 0, ZH // 2), (2, ZH // 2, ZH // 2), (3, 0, 1), (3, 1, 1), (3, 2, ZH - 2))
-PAD = 16
+LANES = 128
 POWER, TOP = 12, 10.5
 
 
@@ -24,27 +24,30 @@
     x4 = x2 * x2
     code = x4 * x4 * x4
     code = jnp.where(x < 0, -code, code).astype(jnp.bfloat16)
-    return code, jnp.broadcast_to(scale, (PAD, values.shape[1])).astype(jnp.bfloat16)
-
-
-def unpacked(ref, rows):
-    scale = ref[pl.ds(rows, PAD), :].astype(jnp.float32)[0:1]
-    code = ref[pl.ds(0, rows), :].astype(jnp.float32)
+    return code, jnp.broadcast_to(scale, (1, LANES))
+
+
+def unpacked(code, scale):
+    code = code.astype(jnp.float32)
+    scale = jnp.concatenate([scale] * (code.shape[1] // LANES), axis=1)
     size = jnp.exp2(jnp.log2(jnp.maximum(jnp.abs(code), 1e-37)) * (1.0 / POWER) - scale)
     return jnp.where(code > 0, size, jnp.where(code < 0, -size, 0.0))
 
 
 def kernel(
     sizes, a_hbm, t_hbm, gram_ref, cross_ref,
-    a_ref, t_ref, at_ref, g_ref, ysend, yrecv, yown, ysum, asend, arecv, asum, brecv, fin,
+    a_ref, t_ref, at_ref, g_ref, ysend, yrecv, yown, asend, arecv, aown, bsend, brecv, bown, fin,
+    yexp, yexps, aexp, aexps, bexp, bexps,
     in_sem, gs_sem, gr_sem, fs_sem, fr_sem, cs_sem, cr_sem, ys_sem, yr_sem, as_sem, ar_sem, bs_sem, br_sem,
-    near_sem, far_sem,
+    ye_sem, yf_sem, ae_sem, af_sem, be_sem, bf_sem, near_sem, far_sem,
 ):
     nx, ny, zh, zl = sizes
     tok, feat = lax.axis_index("tok"), lax.axis_index("feat")
     x, core = feat // 2, lax.rem(feat, 2)
     y, z = tok // (zh * zl), lax.rem(tok, zh * zl)
-    h, l = z // zl, lax.rem(z, zl)
+    shift = zl // 2 * core
+    turned = lax.rem(z + shift, zh * zl)
+    h, l = turned // zl, lax.rem(turned, zl)
     tokens, feats = a_ref.shape
     half, quarter = tokens // 2, tokens // 4
     width = t_ref.shape[0]
@@ -54,6 +57,7 @@
         xx = lax.rem(x + dx + nx, nx)
         yy = lax.rem(y + dy, ny)
         zz = lax.rem(h + dh, zh) * zl + lax.rem(l + dl, zl)
+        zz = lax.rem(zz + zh * zl - shift, zh * zl)
         return {"tok": yy * (zh * zl) + zz, "feat": xx * 2 + on}
 
     partner = at(on=1 - core)
@@ -78,6 +82,12 @@
     def _():
         pl.semaphore_signal(barrier, inc=1, device_id=partner, device_id_type=MESH)
 
+    first.wait()
+    mine.wait()
+    own = g_ref.at[OWN, core]
+    own[:, pl.ds(0, width)] = a_ref[:, pl.ds(0, width)]
+    own[:, pl.ds(width, width)] = t_ref[...].T
+
     @pl.when(core == 1)
     def _():
         pl.semaphore_wait(barrier, 2 * len(near) + 1)
@@ -97,12 +107,6 @@
         def _():
             pl.semaphore_wait(far_sem, 1)
 
-    first.wait()
-    mine.wait()
-    own = g_ref.at[OWN, core]
-    own[:, pl.ds(0, width)] = a_ref[:, pl.ds(0, width)]
-    own[:, pl.ds(width, width)] = t_ref[...].T
-
     def remote(src, dst, send, recv, peer):
         return pltpu.make_async_remote_copy(
             src_ref=src, dst_ref=dst, send_sem=send, recv_sem=recv, device_id=peer, device_id_type=MESH)
@@ -166,10 +170,41 @@
 
     lax.fori_loop(0, feats // tile, transpose, 0)
 
-    def ycopy(p, k):
-        part = pl.ds(0, PIECES[p][2] * zl * brows + PAD)
-        return remote(ysend.at[p, k - 1, part], yrecv.at[p, k - 1, part],
-                      ys_sem.at[p, k - 1], yr_sem.at[p, k - 1], at(dy=k))
+    def ycopies(p, k):
+        part = pl.ds(0, PIECES[p][2] * zl * brows)
+        return (remote(ysend.at[p, k - 1, part], yrecv.at[p, k - 1, part],
+                       ys_sem.at[p, k - 1], yr_sem.at[p, k - 1], at(dy=k)),
+                remote(yexp.at[p * (ny - 1) + k - 1], yexps.at[p * (ny - 1) + k - 1],
+                       ye_sem.at[p, k - 1], yf_sem.at[p, k - 1], at(dy=k)))
+
+    def acopies(p, k):
+        size = PIECES[p][2] * brows
+        there = pl.ds(pl.multiple_of(lax.rem(l + k, zl) * size, brows), size)
+        return (remote(asend.at[p, there], arecv.at[p, k - 1, pl.ds(0, size)],
+                       as_sem.at[p, k - 1], ar_sem.at[p, k - 1], at(dl=k)),
+                remote(aexp.at[p], aexps.at[p * (zl - 1) + k - 1],
+                       ae_sem.at[p, k - 1], af_sem.at[p, k - 1], at(dl=k)))
+
+    def bcopies(p, k):
+        _, low, count = PIECES[p]
+        place = lax.rem(lax.rem(h + k, zh) - low + zh, zh) if count > 1 else 0
+        there = pl.ds(pl.multiple_of(lax.rem(place, count) * brows, brows), brows)
+        return (remote(bsend.at[p, there], brecv.at[p, k - 1],
+                       bs_sem.at[p, k - 1], br_sem.at[p, k - 1], at(dh=k)),
+                remote(bexp.at[p], bexps.at[p * (zh - 1) + k - 1],
+                       be_sem.at[p, k - 1], bf_sem.at[p, k - 1], at(dh=k)))
+
+    def start(copies):
+        for copy in copies:
+            copy.start()
+
+    def arrive(copies):
+        for copy in copies:
+            copy.wait_recv()
+
+    def leave(copies):
+        for copy in copies:
+            copy.wait_send()
 
     def multiply(p):
         stage, low, count = PIECES[p]
@@ -179,10 +214,14 @@
         at_once = yrows // size
         for first_k in range(0, ny, at_once):
             group = order[first_k : first_k + at_once]
-            block = jnp.concatenate(
-                [at_ref[pl.ds(pl.multiple_of(lax.rem(y + k, ny) * yrows + low * zl * brows, zl * brows), size), :]
-                 for k in group], axis=0)
-            terms = jnp.dot(block, both, preferred_element_type=jnp.float32)
+            parts = []
+            for k in group:
+                base = lax.rem(y + k, ny) * yrows
+                for ll in range(zl):
+                    for g in range(low, low + count):
+                        owner = lax.rem(g * zl + ll + zh * zl - shift, zh * zl)
+                        parts.append(at_ref[pl.ds(pl.multiple_of(base + owner * brows, brows), brows), :])
+            terms = jnp.dot(jnp.concatenate(parts, axis=0), both, preferred_element_type=jnp.float32)
             for i, k in enumerate(group):
                 term = terms[i * size : (i + 1) * size]
                 if k == 0:
@@ -190,61 +229,43 @@
                     continue
                 code, exponent = packed(term)
                 ysend[p, k - 1, pl.ds(0, size), :] = code
-                ysend[p, k - 1, pl.ds(size, PAD), :] = exponent
-                ycopy(p, k).start()
-
-    def acopy(p, k):
-        part = pl.ds(0, PIECES[p][2] * brows + PAD)
-        return remote(asend.at[p, k - 1, part], arecv.at[p, k - 1, part],
-                      as_sem.at[p, k - 1], ar_sem.at[p, k - 1], at(dl=k))
-
-    def slots(p, ll):
-        return jnp.concatenate(
-            [ysum[pl.ds(pl.multiple_of((g * zl + ll) * brows, brows), brows), :] for g in range(PIECES[p][2])], axis=0)
+                yexp[p * (ny - 1) + k - 1] = exponent
+                start(ycopies(p, k))
 
     def sum_y(p):
         size, asize = PIECES[p][2] * zl * brows, PIECES[p][2] * brows
         total = yown[p, pl.ds(0, size), :]
         for k in range(1, ny):
-            ycopy(p, k).wait_recv()
-            total += unpacked(yrecv.at[p, k - 1], size)
-        ysum[pl.ds(0, size), :] = total
+            arrive(ycopies(p, k))
+            total += unpacked(yrecv[p, k - 1, pl.ds(0, size), :], yexps[p * (ny - 1) + k - 1])
+        code, exponent = packed(total)
+        asend[p, pl.ds(0, size), :] = code
+        aexp[p] = exponent
         if p == 0:
             meet_far()
         for k in range(1, zl):
-            code, exponent = packed(slots(p, lax.rem(l + k, zl)))
-            asend[p, k - 1, pl.ds(0, asize), :] = code
-            asend[p, k - 1, pl.ds(asize, PAD), :] = exponent
-            acopy(p, k).start()
-        asum[p, pl.ds(0, asize), :] = slots(p, l)
+            start(acopies(p, k))
+        yown[p, pl.ds(0, size), :] = total
+        aown[p, pl.ds(0, asize), :] = yown[p, pl.ds(pl.multiple_of(l * asize, brows), asize), :]
 
     def inside(p, g):
         _, low, count = PIECES[p]
         return (g >= low) & (g < low + count)
 
-    def bcopy(p, k):
-        _, low, count = PIECES[p]
-        there = lax.rem(lax.rem(h + k, zh) - low + zh, zh)
-        if count == 1:
-            there = 0
-        part = pl.ds(pl.multiple_of(there * brows, brows), brows)
-        return remote(asum.at[p, part], brecv.at[p, k - 1], bs_sem.at[p, k - 1], br_sem.at[p, k - 1], at(dh=k))
-
-    def brecvd(p, k):
-        part = pl.ds(0, brows)
-        return remote(asum.at[p, part], brecv.at[p, k - 1], bs_sem.at[p, k - 1], br_sem.at[p, k - 1], at(dh=k))
-
     def sum_a(p):
         asize = PIECES[p][2] * brows
-        total = asum[p, pl.ds(0, asize), :]
+        total = aown[p, pl.ds(0, asize), :]
         for k in range(1, zl):
-            acopy(p, k).wait_recv()
-            total += unpacked(arecv.at[p, k - 1], asize)
-        asum[p, pl.ds(0, asize), :] = total
+            arrive(acopies(p, k))
+            total += unpacked(arecv[p, k - 1, pl.ds(0, asize), :], aexps[p * (zl - 1) + k - 1])
+        code, exponent = packed(total)
+        bsend[p, pl.ds(0, asize), :] = code
+        bexp[p] = exponent
         for k in range(1, zh):
             @pl.when(inside(p, lax.rem(h + k, zh)))
             def _():
-                bcopy(p, k).start()
+                start(bcopies(p, k))
+        bown[p, pl.ds(0, asize), :] = total
 
     def sum_b(p):
         stage, low, count = PIECES[p]
@@ -252,20 +273,20 @@
         @pl.when(inside(p, h))
         def _():
             mine = lax.rem(h - low + zh, zh) if count > 1 else 0
-            total = asum[p, pl.ds(pl.multiple_of(mine * brows, brows), brows), :]
+            total = bown[p, pl.ds(pl.multiple_of(lax.rem(mine, count) * brows, brows), brows), :]
             for k in range(1, zh):
-                brecvd(p, k).wait_recv()
-                total += brecv[p, k - 1]
+                arrive(bcopies(p, k))
+                total += unpacked(brecv[p, k - 1], bexps[p * (zh - 1) + k - 1])
             fin[stage] = total
 
     def sent_b(p):
         for k in range(1, zh):
             @pl.when(inside(p, lax.rem(h + k, zh)))
             def _():
-                brecvd(p, k).wait_send()
-
-    def finish(shift, places):
-        chip = lax.rem(x + shift, nx)
+                leave(bcopies(p, k))
+
+    def finish(dx, places):
+        chip = lax.rem(x + dx, nx)
         columns = pl.ds(pl.multiple_of(chip * 2 * width, 2 * width), 2 * width)
         for out, skip in ((gram_ref, 0), (cross_ref, width)):
             out[:, columns] = jnp.concatenate(
@@ -303,7 +324,6 @@
     multiply(6)
     sum_y(2)
     sum_a(1)
-    sum_b(0)
     sum_y(3)
     sum_y(4)
     sum_a(2)
@@ -312,9 +332,10 @@
     sum_a(4)
     sum_y(6)
     sum_a(5)
-    sum_b(1)
+    sum_b(0)
     finish(0, ((0, 0), (0, 1)))
     sum_a(6)
+    sum_b(1)
     sum_b(2)
     sum_b(3)
     finish(nx - 1, ((1, 0), (2, 0)))
@@ -334,9 +355,9 @@
             across(slot, b).wait_send()
     for p in range(len(PIECES)):
         for k in range(1, ny):
-            ycopy(p, k).wait_send()
+            leave(ycopies(p, k))
         for k in range(1, zl):
-            acopy(p, k).wait_send()
+            leave(acopies(p, k))
         sent_b(p)
 
 
@@ -358,19 +379,29 @@
             pltpu.VMEM((width, tokens), jnp.bfloat16),
             pltpu.VMEM((feats, tokens), jnp.bfloat16),
             pltpu.VMEM((4, 2, tokens, 2 * width), jnp.bfloat16),
-            pltpu.VMEM((n, ny - 1, yrows + PAD, two), jnp.bfloat16),
-            pltpu.VMEM((n, ny - 1, yrows + PAD, two), jnp.bfloat16),
+            pltpu.VMEM((n, ny - 1, yrows, two), jnp.bfloat16),
+            pltpu.VMEM((n, ny - 1, yrows, two), jnp.bfloat16),
             pltpu.VMEM((n, yrows, two), jnp.float32),
-            pltpu.VMEM((yrows, two), jnp.float32),
-            pltpu.VMEM((n, zl - 1, arows + PAD, two), jnp.bfloat16),
-            pltpu.VMEM((n, zl - 1, arows + PAD, two), jnp.bfloat16),
+            pltpu.VMEM((n, yrows, two), jnp.bfloat16),
+            pltpu.VMEM((n, zl - 1, arows, two), jnp.bfloat16),
             pltpu.VMEM((n, arows, two), jnp.float32),
-            pltpu.VMEM((n, zh - 1, brows, two), jnp.float32),
+            pltpu.VMEM((n, arows, two), jnp.bfloat16),
+            pltpu.VMEM((n, zh - 1, brows, two), jnp.bfloat16),
+            pltpu.VMEM((n, arows, two), jnp.float32),
             pltpu.VMEM((4, brows, two), jnp.float32),
+            pltpu.VMEM((n * (ny - 1), 1, LANES), jnp.float32),
+            pltpu.VMEM((n * (ny - 1), 1, LANES), jnp.float32),
+            pltpu.VMEM((n, 1, LANES), jnp.float32),
+            pltpu.VMEM((n * (zl - 1), 1, LANES), jnp.float32),
+            pltpu.VMEM((n, 1, LANES), jnp.float32),
+            pltpu.VMEM((n * (zh - 1), 1, LANES), jnp.float32),
             dma((3,)),
             dma((2, 2)), dma((2, 2)),
             dma((2, 2)), dma((2, 2)),
             dma((4, 2)), dma((4, 2)),
+            dma((n, ny - 1)), dma((n, ny - 1)),
+            dma((n, zl - 1)), dma((n, zl - 1)),
+            dma((n, zh - 1)), dma((n, zh - 1)),
             dma((n, ny - 1)), dma((n, ny - 1)),
             dma((n, zl - 1)), dma((n, zl - 1)),
             dma((n, zh - 1)), dma((n, zh - 1)),

time: 66 us -> 59.4 us (0.900)
  the two profiles are of different devices: /device:TPU:224 before, /device:TPU:1 now
where the time goes in v4:
time: 59.4 us; the launch traced here: 59.2 us
  Pallas kernels  56.4 us (95%)
  local copies, waits for them, and re-layouts  2.17 us (4%)
  between operations  0.65 us (1%)
    pallas_call x1, Pallas kernels, shards(): pl.pallas_call(functools.partial(kernel, sizes), out_shape=(out, out), in...  56.4 us
    unnamed x4, local copies, waits for them, and re-layouts  2.17 us

profile of v4, /device:TPU:1, one launch (start us, length us, event | category | flops | bytes accessed | tf_op | source)
XLA Modules:
  0.0 59.2 jit_solution(11348376512523794991)
XLA Ops:
  0.6 0.0 copy-start
  0.6 0.9 %copy-done = bf16[2048,64]{0,1:T(8,128)(2,1)S(1)} copy-done((bf16[2048,64]{0,1:T(8,128)(2,1)S(1)}, bf16[2048,64]{0,1:T(8,128)(2,1)}, u32[]{:S(2)}) %copy-start) | copy-done | bytes 262168
  1.6 56.4 %shard_map.41 = (f32[16,512]{1,0:T(8,128)S(1)}, f32[16,512]{1,0:T(8,128)S(1)}) custom-call(bf16[2048,1024]{1,0:T(8,128)(2,1)} %a_hbm.1, bf16[64,2048]{1,0:T(8,128)(2,1)S(1)} %bitcast.1), custom_call_target="tpu_custom_call" | custom-call | flops 4294967296 | bytes 4194304 | tf_op jit(solution)/shard_map/pallas_call | solution.py:372
  58.0 0.6 %copy.6 = f32[16,512]{1,0:T(8,128)} copy(f32[16,512]{1,0:T(8,128)S(1)} %get-tuple-element.4) | data formatting | bytes 65536
  58.6 0.6 %copy.7 = f32[16,512]{1,0:T(8,128)} copy(f32[16,512]{1,0:T(8,128)S(1)} %get-tuple-element.5) | data formatting | bytes 65536
Async XLA Ops:
  0.6 1.0 %copy-start = (bf16[2048,64]{0,1:T(8,128)(2,1)S(1)}, bf16[2048,64]{0,1:T(8,128)(2,1)}, u32[]{:S(2)}) copy-start(bf16[2048,64]{0,1:T(8,128)(2,1)} %param.3) | copy-start | bytes 786436

commit v5 on v4

--- a/solution.py
+++ b/solution.py
@@ -68,7 +68,6 @@
         a_ref.at[:, pl.ds(2 * width, feats - 2 * width)], in_sem.at[2])
     first.start()
     mine.start()
-    rest.start()
 
     barrier = pltpu.get_barrier_semaphore()
     near = [dict(dx=1), dict(dx=-1)] + [dict(dy=k) for k in range(1, ny)]
@@ -84,9 +83,9 @@
 
     first.wait()
     mine.wait()
+    rest.start()
     own = g_ref.at[OWN, core]
-    own[:, pl.ds(0, width)] = a_ref[:, pl.ds(0, width)]
-    own[:, pl.ds(width, width)] = t_ref[...].T
+    own[...] = jnp.concatenate([a_ref[:, pl.ds(0, width)], t_ref[...].T], axis=1)
 
     @pl.when(core == 1)
     def _():
@@ -320,18 +319,18 @@
     for b in range(2):
         crossed(OPP, b).wait_recv()
     multiply(4)
+    sum_y(2)
     multiply(5)
     multiply(6)
-    sum_y(2)
+    sum_y(3)
     sum_a(1)
-    sum_y(3)
     sum_y(4)
     sum_a(2)
     sum_y(5)
     sum_a(3)
     sum_a(4)
+    sum_a(5)
     sum_y(6)
-    sum_a(5)
     sum_b(0)
     finish(0, ((0, 0), (0, 1)))
     sum_a(6)
@@ -408,7 +407,7 @@
             pltpu.SemaphoreType.REGULAR, pltpu.SemaphoreType.REGULAR,
         ],
         compiler_params=pltpu.CompilerParams(
-            collective_id=0, has_side_effects=True, vmem_limit_bytes=53 * 1024 * 1024),
+            collective_id=0, has_side_effects=True, vmem_limit_bytes=55104 * 1024),
         cost_estimate=pl.CostEstimate(
             flops=2 * tokens * feats * nx * 4 * width, bytes_accessed=2 * tokens * feats, transcendentals=0),
     )(activations, targets.T)

time: 59.4 us -> 58 us (0.976); the launches traced: 59.2 us -> 57 us
  Pallas kernels: 56.4 us -> 55.1 us
  local copies, waits for them, and re-layouts: 2.17 us -> 1.23 us
    pallas_call x1, Pallas kernels: 56.4 us -> 55.1 us  [shards(): pl.pallas_call(functools.partial(kernel, sizes), out_shape=(out, out), in...]
    unnamed x4 -> x2, local copies, waits for them, and re-layouts: 2.17 us -> 1.23 us
where the time goes in v5:
time: 58 us; the launch traced here: 57 us
  Pallas kernels  55.1 us (95%)
  local copies, waits for them, and re-layouts  1.23 us (2%)
  between operations  0.64 us (1%)
    pallas_call x1, Pallas kernels, shards(): pl.pallas_call(functools.partial(kernel, sizes), out_shape=(out, out), in...  55.1 us
    unnamed x2, local copies, waits for them, and re-layouts  1.23 us

profile of v5, /device:TPU:1, one launch (start us, length us, event | category | flops | bytes accessed | tf_op | source)
XLA Modules:
  0.0 57.0 jit_solution(5184251148711016669)
XLA Ops:
  0.6 55.1 %shard_map.41 = (f32[16,512]{1,0:T(8,128)S(1)}, f32[16,512]{1,0:T(8,128)S(1)}) custom-call(bf16[2048,1024]{1,0:T(8,128)(2,1)} %a_hbm.1, bf16[64,2048]{1,0:T(8,128)(2,1)} %bitcast.1), custom_call_target="tpu_custom_call" | custom-call | flops 4294967296 | bytes 4194304 | tf_op jit(solution)/shard_map/pallas_call | solution.py:371
  55.7 0.6 %copy.6 = f32[16,512]{1,0:T(8,128)} copy(f32[16,512]{1,0:T(8,128)S(1)} %get-tuple-element.4) | data formatting | bytes 65536
  56.3 0.6 %copy.7 = f32[16,512]{1,0:T(8,128)} copy(f32[16,512]{1,0:T(8,128)S(1)} %get-tuple-element.5) | data formatting | bytes 65536

commit v6 on v5

--- a/solution.py
+++ b/solution.py
@@ -13,6 +13,7 @@
 STAGES = (((OWN, 0), (OWN, 1)), ((LEFT, 0), (RIGHT, 0)), ((LEFT, 1), (RIGHT, 1)), ((OPP, 0), (OPP, 1)))
 PIECES = ((0, 0, ZH), (1, 0, ZH), (2, 0, ZH // 2), (2, ZH // 2, ZH // 2), (3, 0, 1), (3, 1, 1), (3, 2, ZH - 2))
 LANES = 128
+PAD = 16
 POWER, TOP = 12, 10.5
 
 
@@ -24,22 +25,24 @@
     x4 = x2 * x2
     code = x4 * x4 * x4
     code = jnp.where(x < 0, -code, code).astype(jnp.bfloat16)
-    return code, jnp.broadcast_to(scale, (1, LANES))
-
-
-def unpacked(code, scale):
-    code = code.astype(jnp.float32)
-    scale = jnp.concatenate([scale] * (code.shape[1] // LANES), axis=1)
+    exponent = jnp.broadcast_to(scale, (PAD, LANES)).astype(jnp.bfloat16)
+    return jnp.concatenate([code[:, :LANES], code[:, LANES:], exponent], axis=0)
+
+
+def unpacked(sent):
+    rows = (sent.shape[0] - PAD) // 2
+    sent = sent.astype(jnp.float32)
+    code, scale = sent[: 2 * rows], sent[2 * rows : 2 * rows + 1]
     size = jnp.exp2(jnp.log2(jnp.maximum(jnp.abs(code), 1e-37)) * (1.0 / POWER) - scale)
-    return jnp.where(code > 0, size, jnp.where(code < 0, -size, 0.0))
+    values = jnp.where(code > 0, size, jnp.where(code < 0, -size, 0.0))
+    return jnp.concatenate([values[:rows], values[rows:]], axis=1)
 
 
 def kernel(
-    sizes, a_hbm, t_hbm, gram_ref, cross_ref,
+    sizes, a_hbm, t_hbm, out_ref,
     a_ref, t_ref, at_ref, g_ref, ysend, yrecv, yown, asend, arecv, aown, bsend, brecv, bown, fin,
-    yexp, yexps, aexp, aexps, bexp, bexps,
     in_sem, gs_sem, gr_sem, fs_sem, fr_sem, cs_sem, cr_sem, ys_sem, yr_sem, as_sem, ar_sem, bs_sem, br_sem,
-    ye_sem, yf_sem, ae_sem, af_sem, be_sem, bf_sem, near_sem, far_sem,
+    near_sem, far_sem,
 ):
     nx, ny, zh, zl = sizes
     tok, feat = lax.axis_index("tok"), lax.axis_index("feat")
@@ -74,8 +77,6 @@
     far = [dict(dl=k) for k in range(1, zl)] + [dict(dh=k) for k in range(1, zh)]
     for there in near:
         pl.semaphore_signal(barrier, inc=1, device_id=at(on=1, **there), device_id_type=MESH)
-    for there in far:
-        pl.semaphore_signal(barrier, inc=1, device_id=at(on=0, **there), device_id_type=MESH)
 
     @pl.when(core == 0)
     def _():
@@ -142,13 +143,14 @@
         return remote(block, block, cs_sem.at[slot, b], cr_sem.at[slot, b], partner)
 
     share(1 - core).start()
-    share(core).start()
 
     @pl.when(core == 0)
     def _():
         hop(LEFT, 0).start()
         hop(RIGHT, 0).start()
 
+    share(core).start()
+
     shared(core).wait_recv()
 
     @pl.when(core == 1)
@@ -158,6 +160,8 @@
 
     hop(LEFT, 1).start()
     hop(RIGHT, 1).start()
+    for there in far:
+        pl.semaphore_signal(barrier, inc=1, device_id=at(on=0, **there), device_id_type=MESH)
 
     rest.wait()
     tile = 128
@@ -169,41 +173,20 @@
 
     lax.fori_loop(0, feats // tile, transpose, 0)
 
-    def ycopies(p, k):
-        part = pl.ds(0, PIECES[p][2] * zl * brows)
-        return (remote(ysend.at[p, k - 1, part], yrecv.at[p, k - 1, part],
-                       ys_sem.at[p, k - 1], yr_sem.at[p, k - 1], at(dy=k)),
-                remote(yexp.at[p * (ny - 1) + k - 1], yexps.at[p * (ny - 1) + k - 1],
-                       ye_sem.at[p, k - 1], yf_sem.at[p, k - 1], at(dy=k)))
-
-    def acopies(p, k):
-        size = PIECES[p][2] * brows
-        there = pl.ds(pl.multiple_of(lax.rem(l + k, zl) * size, brows), size)
-        return (remote(asend.at[p, there], arecv.at[p, k - 1, pl.ds(0, size)],
-                       as_sem.at[p, k - 1], ar_sem.at[p, k - 1], at(dl=k)),
-                remote(aexp.at[p], aexps.at[p * (zl - 1) + k - 1],
-                       ae_sem.at[p, k - 1], af_sem.at[p, k - 1], at(dl=k)))
-
-    def bcopies(p, k):
+    def ycopy(p, k):
+        part = pl.ds(0, 2 * PIECES[p][2] * zl * brows + PAD)
+        return remote(ysend.at[p, k - 1, part], yrecv.at[p, k - 1, part],
+                      ys_sem.at[p, k - 1], yr_sem.at[p, k - 1], at(dy=k))
+
+    def acopy(p, k):
+        part = pl.ds(0, 2 * PIECES[p][2] * brows + PAD)
+        return remote(asend.at[p, lax.rem(l + k, zl), part], arecv.at[p, k - 1, part],
+                      as_sem.at[p, k - 1], ar_sem.at[p, k - 1], at(dl=k))
+
+    def bcopy(p, k):
         _, low, count = PIECES[p]
-        place = lax.rem(lax.rem(h + k, zh) - low + zh, zh) if count > 1 else 0
-        there = pl.ds(pl.multiple_of(lax.rem(place, count) * brows, brows), brows)
-        return (remote(bsend.at[p, there], brecv.at[p, k - 1],
-                       bs_sem.at[p, k - 1], br_sem.at[p, k - 1], at(dh=k)),
-                remote(bexp.at[p], bexps.at[p * (zh - 1) + k - 1],
-                       be_sem.at[p, k - 1], bf_sem.at[p, k - 1], at(dh=k)))
-
-    def start(copies):
-        for copy in copies:
-            copy.start()
-
-    def arrive(copies):
-        for copy in copies:
-            copy.wait_recv()
-
-    def leave(copies):
-        for copy in copies:
-            copy.wait_send()
+        place = lax.rem(lax.rem(lax.rem(h + k, zh) - low + zh, zh), count)
+        return remote(bsend.at[p, place], brecv.at[p, k - 1], bs_sem.at[p, k - 1], br_sem.at[p, k - 1], at(dh=k))
 
     def multiply(p):
         stage, low, count = PIECES[p]
@@ -226,24 +209,21 @@
                 if k == 0:
                     yown[p, pl.ds(0, size), :] = term
                     continue
-                code, exponent = packed(term)
-                ysend[p, k - 1, pl.ds(0, size), :] = code
-                yexp[p * (ny - 1) + k - 1] = exponent
-                start(ycopies(p, k))
+                ysend[p, k - 1, pl.ds(0, 2 * size + PAD), :] = packed(term)
+                ycopy(p, k).start()
 
     def sum_y(p):
         size, asize = PIECES[p][2] * zl * brows, PIECES[p][2] * brows
         total = yown[p, pl.ds(0, size), :]
         for k in range(1, ny):
-            arrive(ycopies(p, k))
-            total += unpacked(yrecv[p, k - 1, pl.ds(0, size), :], yexps[p * (ny - 1) + k - 1])
-        code, exponent = packed(total)
-        asend[p, pl.ds(0, size), :] = code
-        aexp[p] = exponent
+            ycopy(p, k).wait_recv()
+            total += unpacked(yrecv[p, k - 1, pl.ds(0, 2 * size + PAD), :])
+        for ll in range(zl):
+            asend[p, ll, pl.ds(0, 2 * asize + PAD), :] = packed(total[ll * asize : (ll + 1) * asize])
         if p == 0:
             meet_far()
         for k in range(1, zl):
-            start(acopies(p, k))
+            acopy(p, k).start()
         yown[p, pl.ds(0, size), :] = total
         aown[p, pl.ds(0, asize), :] = yown[p, pl.ds(pl.multiple_of(l * asize, brows), asize), :]
 
@@ -255,15 +235,14 @@
         asize = PIECES[p][2] * brows
         total = aown[p, pl.ds(0, asize), :]
         for k in range(1, zl):
-            arrive(acopies(p, k))
-            total += unpacked(arecv[p, k - 1, pl.ds(0, asize), :], aexps[p * (zl - 1) + k - 1])
-        code, exponent = packed(total)
-        bsend[p, pl.ds(0, asize), :] = code
-        bexp[p] = exponent
+            acopy(p, k).wait_recv()
+            total += unpacked(arecv[p, k - 1, pl.ds(0, 2 * asize + PAD), :])
+        for g in range(PIECES[p][2]):
+            bsend[p, g] = packed(total[g * brows : (g + 1) * brows])
         for k in range(1, zh):
             @pl.when(inside(p, lax.rem(h + k, zh)))
             def _():
-                start(bcopies(p, k))
+                bcopy(p, k).start()
         bown[p, pl.ds(0, asize), :] = total
 
     def sum_b(p):
@@ -274,21 +253,21 @@
             mine = lax.rem(h - low + zh, zh) if count > 1 else 0
             total = bown[p, pl.ds(pl.multiple_of(lax.rem(mine, count) * brows, brows), brows), :]
             for k in range(1, zh):
-                arrive(bcopies(p, k))
-                total += unpacked(brecv[p, k - 1], bexps[p * (zh - 1) + k - 1])
+                bcopy(p, k).wait_recv()
+                total += unpacked(brecv[p, k - 1])
             fin[stage] = total
 
     def sent_b(p):
         for k in range(1, zh):
             @pl.when(inside(p, lax.rem(h + k, zh)))
             def _():
-                leave(bcopies(p, k))
+                bcopy(p, k).wait_send()
 
     def finish(dx, places):
         chip = lax.rem(x + dx, nx)
         columns = pl.ds(pl.multiple_of(chip * 2 * width, 2 * width), 2 * width)
-        for out, skip in ((gram_ref, 0), (cross_ref, width)):
-            out[:, columns] = jnp.concatenate(
+        for top, skip in ((0, 0), (brows, width)):
+            out_ref[pl.ds(top, brows), columns] = jnp.concatenate(
                 [fin[stage][:, side * 2 * width + skip : side * 2 * width + skip + width] for stage, side in places],
                 axis=1)
 
@@ -354,9 +333,9 @@
             across(slot, b).wait_send()
     for p in range(len(PIECES)):
         for k in range(1, ny):
-            leave(ycopies(p, k))
+            ycopy(p, k).wait_send()
         for k in range(1, zl):
-            leave(acopies(p, k))
+            acopy(p, k).wait_send()
         sent_b(p)
 
 
@@ -366,41 +345,32 @@
     width = targets.shape[1]
     two, n = 4 * width, len(PIECES)
     yrows, arows, brows = feats // ny, feats // (ny * zl), feats // (ny * zl * zh)
-    out = jax.ShapeDtypeStruct((brows, nx * 2 * width), jnp.float32)
+    out = jax.ShapeDtypeStruct((2 * brows, nx * 2 * width), jnp.float32)
     dma = pltpu.SemaphoreType.DMA
-    return pl.pallas_call(
+    both = pl.pallas_call(
         functools.partial(kernel, sizes),
-        out_shape=(out, out),
+        out_shape=out,
         in_specs=[pl.BlockSpec(memory_space=pl.ANY)] * 2,
-        out_specs=(pl.BlockSpec(memory_space=pltpu.VMEM),) * 2,
+        out_specs=pl.BlockSpec(memory_space=pltpu.VMEM),
         scratch_shapes=[
             pltpu.VMEM((tokens, feats), jnp.bfloat16),
             pltpu.VMEM((width, tokens), jnp.bfloat16),
             pltpu.VMEM((feats, tokens), jnp.bfloat16),
             pltpu.VMEM((4, 2, tokens, 2 * width), jnp.bfloat16),
-            pltpu.VMEM((n, ny - 1, yrows, two), jnp.bfloat16),
-            pltpu.VMEM((n, ny - 1, yrows, two), jnp.bfloat16),
+            pltpu.VMEM((n, ny - 1, 2 * yrows + PAD, LANES), jnp.bfloat16),
+            pltpu.VMEM((n, ny - 1, 2 * yrows + PAD, LANES), jnp.bfloat16),
             pltpu.VMEM((n, yrows, two), jnp.float32),
-            pltpu.VMEM((n, yrows, two), jnp.bfloat16),
-            pltpu.VMEM((n, zl - 1, arows, two), jnp.bfloat16),
+            pltpu.VMEM((n, zl, 2 * arows + PAD, LANES), jnp.bfloat16),
+            pltpu.VMEM((n, zl - 1, 2 * arows + PAD, LANES), jnp.bfloat16),
             pltpu.VMEM((n, arows, two), jnp.float32),
-            pltpu.VMEM((n, arows, two), jnp.bfloat16),
-            pltpu.VMEM((n, zh - 1, brows, two), jnp.bfloat16),
+            pltpu.VMEM((n, zh, 2 * brows + PAD, LANES), jnp.bfloat16),
+            pltpu.VMEM((n, zh - 1, 2 * brows + PAD, LANES), jnp.bfloat16),
             pltpu.VMEM((n, arows, two), jnp.float32),
             pltpu.VMEM((4, brows, two), jnp.float32),
-            pltpu.VMEM((n * (ny - 1), 1, LANES), jnp.float32),
-            pltpu.VMEM((n * (ny - 1), 1, LANES), jnp.float32),
-            pltpu.VMEM((n, 1, LANES), jnp.float32),
-            pltpu.VMEM((n * (zl - 1), 1, LANES), jnp.float32),
-            pltpu.VMEM((n, 1, LANES), jnp.float32),
-            pltpu.VMEM((n * (zh - 1), 1, LANES), jnp.float32),
             dma((3,)),
             dma((2, 2)), dma((2, 2)),
             dma((2, 2)), dma((2, 2)),
             dma((4, 2)), dma((4, 2)),
-            dma((n, ny - 1)), dma((n, ny - 1)),
-            dma((n, zl - 1)), dma((n, zl - 1)),
-            dma((n, zh - 1)), dma((n, zh - 1)),
             dma((n, ny - 1)), dma((n, ny - 1)),
             dma((n, zl - 1)), dma((n, zl - 1)),
             dma((n, zh - 1)), dma((n, zh - 1)),
@@ -411,6 +381,7 @@
         cost_estimate=pl.CostEstimate(
             flops=2 * tokens * feats * nx * 4 * width, bytes_accessed=2 * tokens * feats, transcendentals=0),
     )(activations, targets.T)
+    return both[:brows], both[brows:]
 
 
 def solution(mesh, sizes=(NX, NY, ZH, ZL)):

time: 58 us -> 57.5 us (level); the launches traced: 57 us -> 57.3 us
  Pallas kernels: 55.1 us -> 56 us
  local copies, waits for them, and re-layouts: 1.23 us -> 0.63 us
    unnamed x2 -> x0, local copies, waits for them, and re-layouts: 1.23 us -> none
    pallas_call x1, Pallas kernels: 55.1 us -> 56 us  [shards(): pl.pallas_call(functools.partial(kernel, sizes), out_shape=out, in_specs=...]
    slice x0 -> x1, local copies, waits for them, and re-layouts: none -> 0.63 us  [shards(): return (both[:brows], both[brows:])]
where the time goes in v6:
time: 57.5 us; the launch traced here: 57.3 us
  Pallas kernels  56 us (97%)
  between operations  0.64 us (1%)
  local copies, waits for them, and re-layouts  0.63 us (1%)
    pallas_call x1, Pallas kernels, shards(): pl.pallas_call(functools.partial(kernel, sizes), out_shape=out, in_specs=...  56 us

profile of v6, /device:TPU:1, one launch (start us, length us, event | category | flops | bytes accessed | tf_op | source)
XLA Modules:
  0.0 57.3 jit_solution(5629181556538780297)
XLA Ops:
  0.6 56.0 %shard_map.41 = f32[32,512]{1,0:T(8,128)S(1)} custom-call(bf16[2048,1024]{1,0:T(8,128)(2,1)} %a_hbm.1, bf16[64,2048]{1,0:T(8,128)(2,1)} %bitcast.1), custom_call_target="tpu_custom_call" | custom-call | flops 4294967296 | bytes 4194304 | tf_op jit(solution)/shard_map/pallas_call | solution.py:350
  56.7 0.6 %fusion = (f32[16,512]{1,0:T(8,128)}, f32[16,512]{1,0:T(8,128)}) fusion(f32[32,512]{1,0:T(8,128)S(1)} %shard_map.41), kind=kLoop, calls=%fused_computation | loop fusion | bytes 131072 | tf_op jit(solution)/shard_map/slice | solution.py:384

commit v7 on v6

--- a/solution.py
+++ b/solution.py
@@ -274,8 +274,9 @@
     def take(b):
         for slot in (LEFT, RIGHT):
             hop(slot, b).wait_recv()
+            forward(slot, b).start()
+        for slot in (LEFT, RIGHT):
             across(slot, b).start()
-            forward(slot, b).start()
 
     shared(1 - core).wait_recv()
     multiply(0)

time: 57.5 us -> 57.6 us (level)
  no operation moved by 1% of the time
where the time goes in v7:
time: 57.6 us; the launch traced here: 57 us
  Pallas kernels  55.7 us (97%)
  between operations  0.64 us (1%)
  local copies, waits for them, and re-layouts  0.63 us (1%)
    pallas_call x1, Pallas kernels, shards(): pl.pallas_call(functools.partial(kernel, sizes), out_shape=out, in_specs=...  55.7 us

profile of v7, /device:TPU:1, one launch (start us, length us, event | category | flops | bytes accessed | tf_op | source)
XLA Modules:
  0.0 57.0 jit_solution(2949693278441917046)
XLA Ops:
  0.6 55.7 %shard_map.41 = f32[32,512]{1,0:T(8,128)S(1)} custom-call(bf16[2048,1024]{1,0:T(8,128)(2,1)} %a_hbm.1, bf16[64,2048]{1,0:T(8,128)(2,1)} %bitcast.1), custom_call_target="tpu_custom_call" | custom-call | flops 4294967296 | bytes 4194304 | tf_op jit(solution)/shard_map/pallas_call | solution.py:351
  56.4 0.6 %fusion = (f32[16,512]{1,0:T(8,128)}, f32[16,512]{1,0:T(8,128)}) fusion(f32[32,512]{1,0:T(8,128)S(1)} %shard_map.41), kind=kLoop, calls=%fused_computation | loop fusion | bytes 131072 | tf_op jit(solution)/shard_map/slice | solution.py:385
